TPU v7x, 128 devices: a whole 4x4x4 slice. The times are simulated.
128 devices in a mesh: section: 32 (over y, x, core), expert: 4 (over z).
Axes of the slice: x: 4, y: 4, z: 4, core: 2. Of those that a mesh axis runs over, the one named last changes fastest.
Arguments:
- x_a: bfloat16 [2048, 4096], P('section', 'expert'), may hold values from -6 to 6
- ids_a: int32 [2048, 8], P('section'), may hold values from 0 to 31, all different within a row; in each aligned block of 64 rows (0 to 63, 64 to 127, ...) at most 20 rows name the same one
- prob_a: float32 [2048, 8], P('section'), may hold values from 0.05 to 0.5
- x_b: bfloat16 [2048, 4096], P('section', 'expert'), may hold values from -6 to 6
- ids_b: int32 [2048, 8], P('section'), may hold values from 0 to 31, all different within a row; in each aligned block of 64 rows (0 to 63, 64 to 127, ...) at most 20 rows name the same one
- prob_b: float32 [2048, 8], P('section'), may hold values from 0.05 to 0.5
- cot_b: bfloat16 [2048, 4096], P('section', 'expert'), may hold values from -6 to 6
- w_gate: bfloat16 [32, 4096, 2048], P('section', None, 'expert'), may hold values from -0.09375 to 0.09375
- w_up: bfloat16 [32, 4096, 2048], P('section', None, 'expert'), may hold values from -0.09375 to 0.09375
- w_down: bfloat16 [32, 2048, 4096], P('section', 'expert'), may hold values from -0.125 to 0.125
Outputs:
- out_a: bfloat16 [2048, 4096], P('section', 'expert')
- grad_b: bfloat16 [2048, 4096], P('section', 'expert')
Inputs may be any that keep to these rules, and one draw needn't show every extreme that they name: `ids_a`: each row names 8 different experts. In each aligned block of 64 rows no expert is named more than 20 times, a bound that some block reaches. `ids_b`: as for ids_a.
All inputs are finite; a program needn't handle non-finite values.
Results may differ from a plain program's by a relative error of at most 0.017.
Values may be sent and summed in bfloat16 or wider, within the bound.
No kernel may reach another device: no remote copies, remote signals or barrier semaphores. Data moves between devices by JAX's collectives and lax.ppermute only.
A program may use at most 128 MiB of HBM per device.

v0:
```python
import jax
import jax.numpy as jnp
from jax import lax
from jax.sharding import PartitionSpec as P


def slot_places(idents, experts, capacity):
    flat_ids = idents.reshape(-1)
    onehot = (flat_ids[:, None] == jnp.arange(experts, dtype=jnp.int32)[None, :]).astype(jnp.int32)
    slot_rank = jnp.sum((jnp.cumsum(onehot, axis=0) - 1) * onehot, axis=1)
    return flat_ids * capacity + slot_rank


def slot_buffer(values, places, experts, capacity, top_count):
    row_count = values.shape[0]
    source = jnp.full((experts * capacity,), row_count, jnp.int32)
    source = source.at[places].set(jnp.arange(places.shape[0], dtype=jnp.int32) // top_count)
    padded = jnp.concatenate([values, jnp.zeros((1, values.shape[1]), values.dtype)], axis=0)
    return padded[source].reshape(experts, capacity, values.shape[1])


def combine_slots(returned, places, route_probs):
    flat_rows = returned.reshape(-1, returned.shape[2])
    picked = (
        flat_rows[places]
        .reshape(route_probs.shape[0], route_probs.shape[1], -1)
        .astype(jnp.float32)
    )
    return jnp.einsum("tkd,tk->td", picked, route_probs).astype(jnp.bfloat16)


def on_device(x_a, ids_a, prob_a, x_b, ids_b, prob_b, cot_b, w_gate, w_up, w_down):
    experts = lax.axis_size("section")
    tokens_here, top_count = ids_a.shape
    capacity = min(tokens_here, 5 * tokens_here * top_count // (4 * experts))
    gate_cols = w_gate[0]
    up_cols = w_up[0]
    down_rows = w_down[0]
    contract = (((1,), (1,)), ((), ()))
    places_a = slot_places(ids_a, experts, capacity)
    places_b = slot_places(ids_b, experts, capacity)
    send_a = slot_buffer(x_a, places_a, experts, capacity, top_count)
    whole_rows = lax.all_gather(
        lax.all_to_all(send_a, "section", split_axis=0, concat_axis=0, tiled=True),
        "expert",
        axis=2,
        tiled=True,
    )
    sources, slots, width = whole_rows.shape
    inputs = whole_rows.reshape(sources * slots, width)
    gate_out = jnp.dot(inputs, gate_cols, preferred_element_type=jnp.float32)
    upward = jnp.dot(inputs, up_cols, preferred_element_type=jnp.float32)
    hidden = (jax.nn.silu(gate_out) * upward).astype(jnp.bfloat16)
    partial_value = jnp.dot(hidden, down_rows, preferred_element_type=jnp.float32).reshape(
        sources, slots, width
    )
    result_a = lax.psum_scatter(
        partial_value.astype(jnp.bfloat16), "expert", scatter_dimension=2, tiled=True
    )
    send_b = slot_buffer(x_b, places_b, experts, capacity, top_count)
    send_cot = slot_buffer(cot_b, places_b, experts, capacity, top_count)
    whole_rows = lax.all_gather(
        lax.all_to_all(send_b, "section", split_axis=0, concat_axis=0, tiled=True),
        "expert",
        axis=2,
        tiled=True,
    )
    whole_cots = lax.all_gather(
        lax.all_to_all(send_cot, "section", split_axis=0, concat_axis=0, tiled=True),
        "expert",
        axis=2,
        tiled=True,
    )
    sources, slots, width = whole_rows.shape
    inputs = whole_rows.reshape(sources * slots, width)
    cotangent = whole_cots.reshape(sources * slots, width)
    gate_out = jnp.dot(inputs, gate_cols, preferred_element_type=jnp.float32)
    upward = jnp.dot(inputs, up_cols, preferred_element_type=jnp.float32)
    sigmoid_gate = jax.nn.sigmoid(gate_out)
    hidden_grad = lax.dot_general(
        cotangent, down_rows, contract, preferred_element_type=jnp.float32
    )
    gate_grad = (
        hidden_grad * upward * sigmoid_gate * (1.0 + gate_out * (1.0 - sigmoid_gate))
    ).astype(jnp.bfloat16)
    up_grad = (hidden_grad * gate_out * sigmoid_gate).astype(jnp.bfloat16)
    partial_value = lax.dot_general(
        gate_grad, gate_cols, contract, preferred_element_type=jnp.float32
    )
    partial_value = partial_value + lax.dot_general(
        up_grad, up_cols, contract, preferred_element_type=jnp.float32
    )
    partial_value = partial_value.reshape(sources, slots, width)
    result_b = lax.psum_scatter(
        partial_value.astype(jnp.bfloat16), "expert", scatter_dimension=2, tiled=True
    )
    returned_a = lax.all_to_all(result_a, "section", split_axis=0, concat_axis=0, tiled=True)
    returned_b = lax.all_to_all(result_b, "section", split_axis=0, concat_axis=0, tiled=True)
    return (
        combine_slots(returned_a, places_a, prob_a),
        combine_slots(returned_b, places_b, prob_b),
    )


def solution(mesh):
    in_specs = (
        P("section", "expert"),
        P("section", None),
        P("section", None),
        P("section", "expert"),
        P("section", None),
        P("section", None),
        P("section", "expert"),
        P("section", None, "expert"),
        P("section", None, "expert"),
        P("section", "expert", None),
    )
    out_specs = (P("section", "expert"), P("section", "expert"))
    return jax.shard_map(
        on_device, mesh=mesh, in_specs=in_specs, out_specs=out_specs, check_vma=False
    )
```

profile of v0, /device:TPU:16, one launch (start us, length us, event | category | flops | bytes accessed | tf_op | source)
XLA Modules:
  0.0 417.1 jit_solution(10668220261166945422)
XLA Ops:
  10.6 2.4 scatter_custom_fusion.1
  14.0 2.8 gather_fusion.3
  17.2 27.8 %all_to_all.25 = bf16[32,20,1024]{2,1,0:T(8,128)(2,1)} all-to-all(bf16[32,20,1024]{2,1,0:T(8,128)(2,1)S(1)} %reshape.142), channel_id=1, replica_groups=mesh['section'=32,'expert'=4] {'section'}, dimensions={0} | all-to-all | bytes 2621440 | tf_op jit(solution)/shard_map/all_to_all | solution.py:63
  45.9 2.8 gather_fusion.2
  49.1 26.6 %all_to_all.26 = bf16[32,20,1024]{2,1,0:T(8,128)(2,1)} all-to-all(bf16[32,20,1024]{2,1,0:T(8,128)(2,1)S(1)} %reshape.140), channel_id=1, replica_groups=mesh['section'=32,'expert'=4] {'section'}, dimensions={0} | all-to-all | bytes 2621440 | tf_op jit(solution)/shard_map/all_to_all | solution.py:69
  78.4 2.4 scatter_custom_fusion
  80.9 2.8 gather_fusion
  84.1 26.7 %all_to_all.27 = bf16[32,20,1024]{2,1,0:T(8,128)(2,1)} all-to-all(bf16[32,20,1024]{2,1,0:T(8,128)(2,1)S(1)} %reshape.135), channel_id=1, replica_groups=mesh['section'=32,'expert'=4] {'section'}, dimensions={0} | all-to-all | bytes 2621440 | tf_op jit(solution)/shard_map/all_to_all | solution.py:44
  111.9 7.8 %reshape.143 = bf16[640,4096]{1,0:T(8,128)(2,1)} reshape(bf16[32,20,4096]{2,1,0:T(8,128)(2,1)} %all-gather.8.cloned.1.call-done) | data formatting | bytes 10485760 | tf_op jit(solution)/shard_map/reshape | solution.py:75
  119.7 60.3 %all-gather.6.cloned.1.call-done = bf16[32,20,4096]{2,1,0:T(8,128)(2,1)} async-done(((bf16[32,20,1024]{2,1,0:T(8,128)(2,1)}), bf16[32,20,4096]{2,1,0:T(8,128)(2,1)}) %all-gather.6.cloned.1.call-update) | async-done | bytes 5242896 | tf_op jit(solution)/shard_map/all_gather | solution.py:68
  180.0 7.8 %reshape.141 = bf16[640,4096]{1,0:T(8,128)(2,1)} reshape(bf16[32,20,4096]{2,1,0:T(8,128)(2,1)} %all-gather.6.cloned.1.call-done) | data formatting | bytes 10485760 | tf_op jit(solution)/shard_map/reshape | solution.py:76
  187.9 6.2 %fusion.10 = f32[640,512]{1,0:T(8,128)S(1)} fusion(bf16[640,4096]{1,0:T(8,128)(2,1)} %reshape.143, bf16[1,4096,512]{2,1,0:T(8,128)(2,1)} %param.17), kind=kOutput, calls=%fused_computation.19 | convolution fusion | flops 2684354560 | bytes 10747904 | tf_op jit(solution)/shard_map/dot_general | solution.py:77
  194.1 1.4 copy-done.11
  195.5 2.9 fusion.1
  198.6 3.2 fusion.26
  201.8 2.9 fusion.8
  204.7 7.8 %add_convert_fusion = bf16[640,4096]{1,0:T(8,128)(2,1)} fusion(f32[640,4096]{1,0:T(8,128)S(1)} %fusion.8, bf16[1,4096,512]{2,1,0:T(8,128)(2,1)} %param.18, f32[640,512]{1,0:T(8,128)} %copy-done.4, f32[640,512]{1,0:T(8,128)S(1)} %fusion.10), kind=kOutput, calls=%fused_computation.7 | convolution fusion | flops 2691563520 | bytes 22544384 | tf_op jit(solution)/shard_map/dot_general | solution.py:90
  212.5 7.7 %convert_element_type.44 = bf16[32,20,4096]{2,1,0:T(8,128)(2,1)} reshape(bf16[640,4096]{1,0:T(8,128)(2,1)} %add_convert_fusion) | data formatting | bytes 10485760 | tf_op jit(solution)/shard_map/convert_element_type | solution.py:95
  220.5 27.7 %all-gather.4.cloned.1.call-done = bf16[32,20,4096]{2,1,0:T(8,128)(2,1)} async-done(((bf16[32,20,1024]{2,1,0:T(8,128)(2,1)}), bf16[32,20,4096]{2,1,0:T(8,128)(2,1)}) %all-gather.4.cloned.1.call-update) | async-done | bytes 5242896 | tf_op jit(solution)/shard_map/all_gather | solution.py:43
  248.2 7.7 %reshape.136 = bf16[640,4096]{1,0:T(8,128)(2,1)} reshape(bf16[32,20,4096]{2,1,0:T(8,128)(2,1)} %all-gather.4.cloned.1.call-done) | data formatting | bytes 10485760 | tf_op jit(solution)/shard_map/reshape | solution.py:50
  255.9 6.2 %fusion.12 = f32[640,512]{1,0:T(8,128)S(1)} fusion(bf16[640,4096]{1,0:T(8,128)(2,1)} %reshape.136, bf16[1,4096,512]{2,1,0:T(8,128)(2,1)} %param.17), kind=kOutput, calls=%fused_computation.21 | convolution fusion | flops 2684354560 | bytes 10747904 | tf_op jit(solution)/shard_map/dot_general | solution.py:51
  263.6 3.0 fusion.29
  266.7 6.8 %convolution_convert_fusion = bf16[32,20,4096]{2,0,1:T(8,128)(2,1)} fusion(bf16[1,512,4096]{2,1,0:T(8,128)(2,1)} %param.19, bf16[32,20,512]{2,1,0:T(8,128)(2,1)S(1)} %dot_general.34), kind=kOutput, calls=%fused_computation.8 | convolution fusion | flops 2686976000 | bytes 10092544 | tf_op jit(solution)/shard_map/dot_general | solution.py:54
  273.5 41.7 %reduce-scatter.5.cloned.1.call-done = bf16[32,20,1024]{2,1,0:T(8,128)(2,1)} async-done(((bf16[32,20,4096]{2,1,0:T(8,128)(2,1)}), bf16[32,20,1024]{2,1,0:T(8,128)(2,1)}) %reduce-scatter.5.cloned.1.call-update) | async-done | bytes 1310736 | tf_op jit(solution)/shard_map/reduce_scatter | solution.py:94
  315.2 7.4 %all-to-all-start.4 = ((bf16[32,20,1024]{2,1,0:T(8,128)(2,1)}), bf16[32,20,1024]{2,1,0:T(8,128)(2,1)S(1)}, u32[]{:S(2)}, u32[]{:S(2)}) async-start(bf16[32,20,1024]{2,1,0:T(8,128)(2,1)} %reduce-scatter.5.cloned.1.call-done), calls=%async_computation.6 | async-start | bytes 3145728 | tf_op jit(solution)/shard_map/all_to_all | solution.py:98
  322.6 50.1 %reduce-scatter.3.cloned.1.call-done = bf16[32,20,1024]{2,0,1:T(8,128)(2,1)} async-done(((bf16[32,20,4096]{2,0,1:T(8,128)(2,1)}), bf16[32,20,1024]{2,0,1:T(8,128)(2,1)}) %reduce-scatter.3.cloned.1.call-update) | async-done | bytes 1310736 | tf_op jit(solution)/shard_map/reduce_scatter | solution.py:57
  372.6 3.2 copy.28
  375.9 7.6 %all-to-all-start.1 = ((bf16[32,20,1024]{2,1,0:T(8,128)(2,1)}), bf16[32,20,1024]{2,1,0:T(8,128)(2,1)}, u32[]{:S(2)}, u32[]{:S(2)}) async-start(bf16[32,20,1024]{2,1,0:T(8,128)(2,1)} %copy.28), calls=%async_computation.2 | async-start | bytes 3145728 | tf_op jit(solution)/shard_map/all_to_all | solution.py:97
  384.0 2.1 gather_fusion.4
  386.5 18.5 %all-to-all-done.1 = bf16[32,20,1024]{2,1,0:T(8,128)(2,1)} async-done(((bf16[32,20,1024]{2,1,0:T(8,128)(2,1)}), bf16[32,20,1024]{2,1,0:T(8,128)(2,1)}, u32[]{:S(2)}, u32[]{:S(2)}) %all-to-all-start.1) | async-done | bytes 1310752 | tf_op jit(solution)/shard_map/all_to_all | solution.py:97
  405.0 2.3 reshape.137
  407.3 2.1 gather_fusion.1
  (86 shorter events, 14.2 us)
Async XLA Ops:
  7.2 104.8 %all-gather.8.cloned.1.call-start = ((), (), s32[]{:S(2)}) async-start(), calls=%async_computation.10 | async-start | bytes 7864320 | tf_op jit(solution)/shard_map/all_gather | solution.py:62
  45.0 0.9 copy-start.5
  45.0 135.0 %all-gather.6.cloned.1.call-start = ((), (), s32[]{:S(2)}) async-start(), calls=%async_computation.9 | async-start | bytes 7864320 | tf_op jit(solution)/shard_map/all_gather | solution.py:68
  75.7 0.7 copy-start.7
  75.7 5.2 %copy-start.6 = (bf16[64,1024]{1,0:T(8,128)(2,1)S(1)}, bf16[64,1024]{1,0:T(8,128)(2,1)}, u32[]{:S(2)}) copy-start(bf16[64,1024]{1,0:T(8,128)(2,1)} %param.10) | copy-start | bytes 393220
  75.7 172.4 %all-gather.4.cloned.1.call-start = ((), (), s32[]{:S(2)}) async-start(), calls=%async_computation.7 | async-start | bytes 7864320 | tf_op jit(solution)/shard_map/all_gather | solution.py:43
  110.8 204.4 %reduce-scatter.5.cloned.1.call-start = ((), (), s32[]{:S(2)}) async-start(), calls=%async_computation.11 | async-start | bytes 7864320 | tf_op jit(solution)/shard_map/reduce_scatter | solution.py:94
  180.0 18.4 %slice-start = ((s8[5242880]{0:T(1024)(128)(4,1)}), s8[1048576]{0:T(1024)(128)(4,1)S(1)}, s32[]{:S(2)}) async-start(s8[5242880]{0:T(1024)(128)(4,1)} %bitcast.86), calls=%async_computation.12 | async-start | bytes 2097152
  187.9 6.2 %copy-start = (bf16[640,4096]{1,0:T(8,128)(2,1)S(1)}, bf16[640,4096]{1,0:T(8,128)(2,1)}, u32[]{:S(2)}) copy-start(bf16[640,4096]{1,0:T(8,128)(2,1)} %reshape.141) | copy-start | bytes 15728644
  187.9 7.6 %copy-start.11 = (bf16[1,512,4096]{2,1,0:T(8,128)(2,1)S(1)}, bf16[1,512,4096]{2,1,0:T(8,128)(2,1)}, u32[]{:S(2)}) copy-start(bf16[1,512,4096]{2,1,0:T(8,128)(2,1)} %param.19) | copy-start | bytes 12582916
  187.9 10.5 %slice-start.1 = ((s8[5242880]{0:T(1024)(128)(4,1)}), s8[4194304]{0:T(1024)(128)(4,1)S(1)}, s32[]{:S(2)}) async-start(s8[5242880]{0:T(1024)(128)(4,1)} %bitcast.86), calls=%async_computation.13 | async-start | bytes 8388608
  195.5 3.0 copy-start.2
  198.6 3.2 copy-start.4
  198.6 3.2 copy-start.10
  220.2 152.4 %reduce-scatter.3.cloned.1.call-start = ((), (), s32[]{:S(2)}) async-start(), calls=%async_computation.8 | async-start | bytes 6553600 | tf_op jit(solution)/shard_map/reduce_scatter | solution.py:57
  255.9 6.4 %copy-start.1 = (bf16[640,4096]{1,0:T(8,128)(2,1)S(1)}, bf16[640,4096]{1,0:T(8,128)(2,1)}, u32[]{:S(2)}) copy-start(bf16[640,4096]{1,0:T(8,128)(2,1)} %reshape.136) | copy-start | bytes 15728644
  255.9 7.7 %copy-start.3 = (bf16[1,4096,512]{2,1,0:T(8,128)(2,1)S(1)}, bf16[1,4096,512]{2,1,0:T(8,128)(2,1)}, u32[]{:S(2)}) copy-start(bf16[1,4096,512]{2,1,0:T(8,128)(2,1)} %param.18) | copy-start | bytes 12582916
  315.2 60.7 %all-to-all-start.4 = ((bf16[32,20,1024]{2,1,0:T(8,128)(2,1)}), bf16[32,20,1024]{2,1,0:T(8,128)(2,1)S(1)}, u32[]{:S(2)}, u32[]{:S(2)}) async-start(bf16[32,20,1024]{2,1,0:T(8,128)(2,1)} %reduce-scatter.5.cloned.1.call-done), calls=%async_computation.6 | async-start | bytes 3145728 | tf_op jit(solution)/shard_map/all_to_all | solution.py:98
  375.9 7.6 %copy-start.8 = (f32[64,8]{0,1:T(8,128)S(1)}, f32[64,8]{0,1:T(8,128)}, u32[]{:S(2)}) copy-start(f32[64,8]{0,1:T(8,128)} %param.15) | copy-start | bytes 6148
  375.9 7.7 %copy-start.9 = (f32[64,8]{0,1:T(8,128)S(1)}, f32[64,8]{0,1:T(8,128)}, u32[]{:S(2)}) copy-start(f32[64,8]{0,1:T(8,128)} %param.12) | copy-start | bytes 6148
  375.9 29.1 %all-to-all-start.1 = ((bf16[32,20,1024]{2,1,0:T(8,128)(2,1)}), bf16[32,20,1024]{2,1,0:T(8,128)(2,1)}, u32[]{:S(2)}, u32[]{:S(2)}) async-start(bf16[32,20,1024]{2,1,0:T(8,128)(2,1)} %copy.28), calls=%async_computation.2 | async-start | bytes 3145728 | tf_op jit(solution)/shard_map/all_to_all | solution.py:97
Sparse Core Ops, SparseCore 0:
  45.1 66.7 all-gather.7
  113.6 66.4 all-gather.5
  181.7 66.4 all-gather.3
  250.4 64.7 reduce-scatter.4
  317.4 55.1 reduce-scatter.2
where the time goes:
time: 421 us; the launch traced here: 417 us
  waiting for transfers between devices  199 us (47%)
  blocking collectives  81.1 us (19%)
  local copies, waits for them, and re-layouts  63.9 us (15%)
  matrix products  39.8 us (9%)
  starting transfers between devices  15.6 us (4%)
  between operations  14.1 us (3%)
    reduce_scatter x2, waiting for transfers between devices, on_device(): lax.psum_scatter(partial_value.astype(jnp.bfloat16), 'expert', scatter_di...  91.8 us
    all_gather x1, waiting for transfers between devices, on_device(): lax.all_gather(lax.all_to_all(send_cot, 'section', split_axis=0, concat_a...  60.3 us
    all_to_all x1, blocking collectives, on_device(): lax.all_to_all(send_b, 'section', split_axis=0, concat_axis=0, tiled=True)  27.8 us
    all_gather x1, waiting for transfers between devices, on_device(): lax.all_gather(lax.all_to_all(send_a, 'section', split_axis=0, concat_axi...  27.7 us
    all_to_all x1, blocking collectives, on_device(): lax.all_to_all(send_a, 'section', split_axis=0, concat_axis=0, tiled=True)  26.7 us
    all_to_all x1, blocking collectives, on_device(): lax.all_to_all(send_cot, 'section', split_axis=0, concat_axis=0, tiled=True)  26.6 us
    all_to_all x1, waiting for transfers between devices, on_device(): lax.all_to_all(result_a, 'section', split_axis=0, concat_axis=0, tiled=True)  18.5 us
    reshape x2, local copies, waits for them, and re-layouts, on_device(): inputs = whole_rows.reshape(sources * slots, width)  15.5 us
  transfers between devices with their start and end apart: 7, of which 6 were waited for; matrix products, arithmetic and copies ran while one was open for 21% of the time, Pallas kernels for 0%

commit v1 on v0

v1 whole, which is shorter than its diff:
```python
import functools

import jax
import jax.numpy as jnp
from jax import lax
from jax.experimental import pallas as pl
from jax.experimental.pallas import tpu as pltpu
from jax.sharding import PartitionSpec as P

TOK = 64
CAP = 20
HALF = 512
CORES = 2
ROWS = 16 * CAP
GROUP = 4 * TOK
SLOTS = 4 * CAP
META = 128
BASES = (0, 64)
NEAR_A = 0
META_A = HALF
NEAR_B = HALF + META
META_B = 3 * HALF + META
BF16 = jnp.bfloat16
F32 = jnp.float32


def _section_moves(move):
    pairs = []
    for y in range(4):
        for x in range(4):
            for core in range(CORES):
                axis, shift = move[core]
                there_y = (y + shift) % 4 if axis == "y" else y
                there_x = (x + shift) % 4 if axis == "x" else x
                there_core = 1 - core if axis == "core" else core
                pairs.append(((y * 4 + x) * 2 + core, (there_y * 4 + there_x) * 2 + there_core))
    return pairs


def _shifts(axes):
    return [None] + [_section_moves(tuple((a, s) for a in axes)) for s in (1, 2, 3)]


def _groups(axes):
    groups = []
    for core in range(CORES):
        for other in range(4):
            if axes[core] == "y":
                groups.append([(i * 4 + other) * 2 + core for i in range(4)])
            else:
                groups.append([(other * 4 + i) * 2 + core for i in range(4)])
    return groups


FIRST = ("section", _shifts("yx"))
LAST = ("section", _shifts("xy"))
DEPTH = ("expert", [None] + [[(i, (i + s) % 4) for i in range(4)] for s in (1, 2, 3)])
LAST_GROUPS = _groups("xy")
SWAP = _section_moves((("core", 0), ("core", 0)))


def spread(values, ring):
    axis, shifts = ring
    return [values] + [lax.ppermute(values, axis, shifts[4 - d]) for d in (1, 2, 3)]


def collect(parts, ring):
    axis, shifts = ring
    arrived = [lax.ppermute(parts[d], axis, shifts[d]) for d in (1, 2, 3)]
    total = parts[0].astype(F32)
    for part in arrived:
        total = total + part.astype(F32)
    return total.astype(BF16)


def swap(values):
    return lax.ppermute(values, "section", SWAP)


def dot(a, b):
    return jnp.dot(a, b, preferred_element_type=F32)


def dot_last(a, b):
    return lax.dot_general(a, b, (((1,), (1,)), ((), ())), preferred_element_type=F32)


def dot_first(a, b):
    return lax.dot_general(a, b, (((0,), (0,)), ((), ())), preferred_element_type=F32)


def params(mib):
    return pltpu.CompilerParams(vmem_limit_bytes=mib * 2**20)


def cost(flops, moved, transcendentals=0):
    return pl.CostEstimate(flops=flops // 64, bytes_accessed=moved // 64, transcendentals=0)


def slot_matrices(meta, here, sibling):
    rows = lax.broadcasted_iota(jnp.int32, (8, META), 0)
    lanes = lax.broadcasted_iota(jnp.int32, (8, META), 1)
    expert = jnp.where(rows % 2 == 0, here, sibling)
    wanted = jnp.where(rows < 2, BASES[0] + expert, jnp.where(rows < 4, BASES[1] + expert, -1))
    select = (lanes == wanted).astype(F32).astype(BF16)
    routed = (meta.astype(F32) > 0.0).astype(F32).astype(BF16)
    match = dot_last(select, routed)
    before = lax.broadcasted_iota(jnp.int32, (GROUP, GROUP), 0)
    token = lax.broadcasted_iota(jnp.int32, (GROUP, GROUP), 1)
    same = jnp.logical_and(before < token, before // TOK == token // TOK)
    rank = dot(match.astype(BF16), same.astype(F32).astype(BF16))
    block = lax.broadcasted_iota(jnp.int32, (8, GROUP), 1) // TOK
    place = jnp.where(match > 0.5, block * CAP + rank.astype(jnp.int32), -1)
    slot = lax.broadcasted_iota(jnp.int32, (SLOTS, GROUP), 0)
    pieces = [(slot == place[i : i + 1, :]).astype(F32) for i in range(4)]
    return [jnp.concatenate(pieces[i : i + 2], axis=0).astype(BF16) for i in (0, 2)]


def gather_first_kernel(where, *refs):
    parts, (own_ref, sibling_ref, ahead_ref, back_ref) = refs[:4], refs[4:]
    for group in range(4):
        values = parts[group][...]
        meta = values[:, 3 * HALF :]
        ahead, back = slot_matrices(meta, where[1], where[2])
        ahead_ref[group] = ahead
        back_ref[group] = back
        place = slice(group * SLOTS, (group + 1) * SLOTS)
        for slots, begin, end, column in (
            (ahead, 0, HALF, NEAR_A),
            (ahead, 3 * HALF, 3 * HALF + META, META_A),
            (back, HALF, 3 * HALF, NEAR_B),
            (back, 3 * HALF, 3 * HALF + META, META_B),
        ):
            picked = dot(slots, values[:, begin:end]).astype(BF16)
            own_ref[place, column : column + end - begin] = picked[:SLOTS]
            sibling_ref[place, column : column + end - begin] = picked[SLOTS:]


def gather_first(where, parts):
    width = 3 * HALF + 2 * META
    rows = jax.ShapeDtypeStruct((ROWS, width), BF16)
    slots = jax.ShapeDtypeStruct((4, 2 * SLOTS, GROUP), BF16)
    whole = pl.BlockSpec(memory_space=pltpu.VMEM)
    return pl.pallas_call(
        gather_first_kernel,
        in_specs=[pl.BlockSpec(memory_space=pltpu.SMEM)] + [whole] * 4,
        out_specs=[whole] * 4,
        out_shape=[rows, rows, slots, slots],
        compiler_params=params(16),
        cost_estimate=cost(2 * 4 * 2 * SLOTS * GROUP * width, 6 * 2**20),
    )(where, *parts)


def along(where, distance, width):
    start = lax.rem(where[0] + distance, 4) * width
    return pl.ds(pl.multiple_of(start, HALF), HALF)


def gather_last_kernel(where, slots_ref, values_ref, own_ref, sibling_ref):
    for z in range(4):
        values = jnp.concatenate(
            [values_ref[pl.ds((4 * part + z) * TOK, TOK), :] for part in range(4)], axis=0
        )
        picked = dot(slots_ref[0], values).astype(BF16)
        columns = along(where, z, HALF)
        own_ref[:, columns] = picked[:SLOTS]
        sibling_ref[:, columns] = picked[SLOTS:]


def gather_last(where, slots, values):
    tensors = values.shape[1] // HALF
    shape = jax.ShapeDtypeStruct((ROWS, tensors * 4 * HALF), BF16)
    return pl.pallas_call(
        gather_last_kernel,
        grid_spec=pltpu.PrefetchScalarGridSpec(
            num_scalar_prefetch=1,
            grid=(tensors, 4),
            in_specs=[
                pl.BlockSpec((1, 2 * SLOTS, GROUP), lambda t, i, w: (i, 0, 0)),
                pl.BlockSpec((4 * GROUP, HALF), lambda t, i, w: (lax.rem(w[3] + i, 4), t)),
            ],
            out_specs=[pl.BlockSpec((SLOTS, 4 * HALF), lambda t, i, w: (i, t))] * 2,
        ),
        out_shape=[shape, shape],
        compiler_params=params(16),
        cost_estimate=cost(
            2 * 16 * 2 * SLOTS * GROUP * HALF * tensors, 14 * 2**20 * tensors
        ),
    )(where, slots, values)


def scatter_first_kernel(slots_ref, own_ref, sibling_ref, *outs):
    for group in range(4):
        place = slice(group * SLOTS, (group + 1) * SLOTS)
        rows = jnp.concatenate([own_ref[place, :], sibling_ref[place, :]], axis=0)
        outs[group][...] = dot_first(slots_ref[group], rows).astype(BF16)


def scatter_first(slots, own, sibling):
    whole = pl.BlockSpec(memory_space=pltpu.VMEM)
    return pl.pallas_call(
        scatter_first_kernel,
        in_specs=[whole] * 3,
        out_specs=[whole] * 4,
        out_shape=[jax.ShapeDtypeStruct((GROUP, HALF), BF16)] * 4,
        compiler_params=params(16),
        cost_estimate=cost(2 * 4 * 2 * SLOTS * GROUP * HALF, 3 * 2**20),
    )(slots, own, sibling)


def scatter_last_kernel(where, slots_ref, own_ref, sibling_ref, out_ref):
    for z in range(4):
        columns = along(where, z, HALF)
        rows = jnp.concatenate([own_ref[:, columns], sibling_ref[:, columns]], axis=0)
        dense = dot_first(slots_ref[0], rows).astype(BF16)
        for part in range(4):
            out_ref[pl.ds((4 * part + z) * TOK, TOK), :] = dense[part * TOK : (part + 1) * TOK]


def scatter_last(where, slots, own, sibling):
    return pl.pallas_call(
        scatter_last_kernel,
        grid_spec=pltpu.PrefetchScalarGridSpec(
            num_scalar_prefetch=1,
            grid=(4,),
            in_specs=[pl.BlockSpec((1, 2 * SLOTS, GROUP), lambda i, w: (i, 0, 0))]
            + [pl.BlockSpec((SLOTS, 4 * HALF), lambda i, w: (i, 0))] * 2,
            out_specs=pl.BlockSpec((4 * GROUP, HALF), lambda i, w: (lax.rem(w[3] + i, 4), 0)),
        ),
        out_shape=jax.ShapeDtypeStruct((16 * GROUP, HALF), BF16),
        compiler_params=params(16),
        cost_estimate=cost(2 * 16 * 2 * SLOTS * GROUP * HALF, 14 * 2**20),
    )(where, slots, own, sibling)


def lay_out(where, near, last, out_ref):
    for z in range(4):
        out_ref[:, along(where, z, 2 * HALF)] = near[z]
        out_ref[:, (2 * z + 1) * HALF : (2 * z + 2) * HALF] = last[z]


def halves(ref, first=0):
    return [ref[:, first + z * HALF : first + (z + 1) * HALF] for z in range(4)]


def write_result(where, weight, product, near_out, last_out):
    step = pl.program_id(0)
    for z in range(4):
        near_out[z][...] = (product(along(where, z, 2 * HALF)) * weight).astype(BF16)
    for z in range(4):
        value = (product(pl.ds((2 * z + 1) * HALF, HALF)) * weight).astype(BF16)
        for part in range(2):

            @pl.when(step == part)
            def _():
                last_out[part][:, z * HALF : (z + 1) * HALF] = value


def pick(refs):
    return jnp.where(pl.program_id(0) == 0, refs[0][...], refs[1][...])


def slot_weight(rows, base, expert):
    lanes = lax.broadcasted_iota(jnp.int32, (ROWS, META), 1)
    chosen = jnp.logical_or(lanes == base + expert, lanes == base + 32 + expert)
    return jnp.sum(jnp.where(chosen, rows.astype(F32), 0.0), axis=1, keepdims=True)


def forward_kernel(where, *refs):
    near, last, metas, (gate_ref, up_ref, down_ref) = refs[:4], refs[4:6], refs[6:8], refs[8:11]
    near_out, last_out, (values, hidden) = refs[11:15], refs[15:17], refs[17:]
    near = [r[...] for r in near]
    for part in range(2):

        @pl.when(pl.program_id(0) == part)
        def _():
            lay_out(where, near, halves(last[part]), values)

    gate = dot(values[...], gate_ref[0])
    upward = dot(values[...], up_ref[0])
    hidden[...] = (gate / (1.0 + jnp.exp(-gate)) * upward).astype(BF16)
    weight = slot_weight(pick(metas), BASES[0], where[1])

    def product(columns):
        return dot(hidden[...], down_ref[0, :, columns])

    write_result(where, weight, product, near_out, last_out)


def backward_kernel(where, *refs):
    near, last, metas, (gate_ref, up_ref, down_ref) = refs[:4], refs[4:6], refs[6:8], refs[8:11]
    near_out, last_out, (values, cotangent, gate_grad, up_grad) = refs[11:15], refs[15:17], refs[17:]
    for part in range(2):

        @pl.when(pl.program_id(0) == part)
        def _():
            lay_out(where, [r[:, :HALF] for r in near], halves(last[part]), values)
            lay_out(where, [r[:, HALF:] for r in near], halves(last[part], 4 * HALF), cotangent)

    gate = dot(values[...], gate_ref[0])
    upward = dot(values[...], up_ref[0])
    grad = dot_last(cotangent[...], down_ref[0])
    sigmoid = 1.0 / (1.0 + jnp.exp(-gate))
    scaled = grad * sigmoid
    gate_grad[...] = (scaled * upward * (1.0 + gate * (1.0 - sigmoid))).astype(BF16)
    up_grad[...] = (scaled * gate).astype(BF16)
    weight = slot_weight(pick(metas), BASES[1], where[1])

    def product(rows):
        return dot_last(gate_grad[...], gate_ref[0, rows]) + dot_last(up_grad[...], up_ref[0, rows])

    write_result(where, weight, product, near_out, last_out)


def expert_call(backward, where, near, last, rows, w_gate, w_up, w_down):
    wide = w_gate.shape[2]
    column = (META_B if backward else META_A) // META
    once = pl.Buffered(1)
    in_specs = [pl.BlockSpec((ROWS, p.shape[1]), lambda i, w: (i, 0)) for p in near]
    in_specs += [pl.BlockSpec(p.shape, lambda i, w: (0, 0), pipeline_mode=once) for p in last]
    in_specs += [
        pl.BlockSpec((ROWS, META), lambda i, w: (0, column), pipeline_mode=once) for _ in rows
    ]
    weights = [w_gate, w_up, w_down]
    in_specs += [
        pl.BlockSpec(p.shape, lambda i, w: (0, 0, 0), pipeline_mode=once) for p in weights
    ]
    out_specs = [pl.BlockSpec((ROWS, HALF), lambda i, w: (i, 0))] * 4
    out_specs += [
        pl.BlockSpec((ROWS, 4 * HALF), lambda i, w: (0, 0), pipeline_mode=once) for _ in rows
    ]
    out_shape = [jax.ShapeDtypeStruct((2 * ROWS, HALF), BF16)] * 4
    out_shape += [jax.ShapeDtypeStruct((ROWS, 4 * HALF), BF16)] * 2
    laid = pltpu.VMEM((ROWS, 8 * HALF), BF16)
    narrow = pltpu.VMEM((ROWS, wide), BF16)
    products = 5 if backward else 3
    outs = pl.pallas_call(
        backward_kernel if backward else forward_kernel,
        grid_spec=pltpu.PrefetchScalarGridSpec(
            num_scalar_prefetch=1,
            grid=(2,),
            in_specs=in_specs,
            out_specs=out_specs,
            scratch_shapes=[laid, laid, narrow, narrow] if backward else [laid, narrow],
        ),
        out_shape=out_shape,
        compiler_params=params(44 if backward else 34),
        cost_estimate=cost(
            2 * products * 2 * ROWS * 8 * HALF * wide, 30 * 2**20, 2 * ROWS * wide
        ),
    )(where, *near, *last, *rows, *weights)
    return outs[:4], outs[4:]


def weight_columns(idents, weights):
    experts = jnp.arange(32, dtype=jnp.int32)
    table = jnp.sum(
        jnp.where(idents[:, :, None] == experts[None, None, :], weights[:, :, None], 0.0), axis=1
    )
    high = lax.reduce_precision(table, exponent_bits=8, mantissa_bits=7)
    return [high.astype(BF16), (table - high).astype(BF16)]


def on_device(x_a, ids_a, prob_a, x_b, ids_b, prob_b, cot_b, w_gate, w_up, w_down):
    here = lax.axis_index("section").astype(jnp.int32)
    place = lax.axis_index("expert").astype(jnp.int32)
    core = here % 2
    group = jnp.where(core == 0, here // 2 % 4, here // 8)
    where = jnp.stack([place, here, here + 1 - 2 * core, group])
    meta = jnp.concatenate(weight_columns(ids_a, prob_a) + weight_columns(ids_b, prob_b), axis=1)
    inputs = (x_a, x_b, cot_b)
    def stack(parts):
        return jnp.concatenate(parts, axis=0)

    def together(*values):
        return lax.optimization_barrier(values)

    def gather_section(group):
        return lax.all_gather(
            group, "section", axis=0, tiled=True, axis_index_groups=LAST_GROUPS
        )

    def scatter_section(dense):
        return lax.psum_scatter(
            dense, "section", scatter_dimension=0, tiled=True, axis_index_groups=LAST_GROUPS
        )

    def cut(values):
        height = values.shape[0] // 4
        return [values[d * height : (d + 1) * height] for d in range(4)]

    def slot_rows(slots, dense):
        own, sibling = gather_last(where, slots, dense)
        return own, swap(sibling)

    quarters = spread(jnp.concatenate([v[:, HALF:] for v in inputs], axis=1), DEPTH)
    first = spread(jnp.concatenate([v[:, :HALF] for v in inputs] + [meta], axis=1), FIRST)
    quarters, first = together(quarters, first)

    whole_a = spread(stack([q[:, :HALF] for q in quarters]), FIRST)
    near = spread(stack(first), LAST)
    whole_a, near = together(whole_a, near)

    dense_a = gather_section(stack(whole_a))
    own, sibling, slots_a, slots_b = gather_first(where, near)
    whole_b = spread(stack([q[:, HALF:] for q in quarters]), FIRST)
    rows = (own, swap(sibling))
    near_a = spread(stack([r[:, NEAR_A : NEAR_A + HALF] for r in rows]), DEPTH)
    whole_b, near_a = together(whole_b, near_a)

    dense_b = gather_section(stack(whole_b))
    near_b = spread(stack([r[:, NEAR_B : NEAR_B + 2 * HALF] for r in rows]), DEPTH)
    last_a = slot_rows(slots_a, dense_a)
    near_a, (own, sibling) = expert_call(
        False, where, near_a, last_a, rows, w_gate, w_up, w_down
    )
    dense_a = scatter_last(where, slots_a, own, swap(sibling))
    near_b, dense_a = together(near_b, dense_a)

    group_a = scatter_section(dense_a)
    returned_a = collect(near_a, DEPTH)
    last_b = slot_rows(slots_b, dense_b)
    near_b, (own, sibling) = expert_call(True, where, near_b, last_b, rows, w_gate, w_up, w_down)
    dense_b = scatter_last(where, slots_b, own, swap(sibling))
    dense_b, returned_a = together(dense_b, returned_a)

    group_b = scatter_section(dense_b)
    returned_b = collect(near_b, DEPTH)
    parts_a = scatter_first(slots_a, returned_a[:ROWS], swap(returned_a[ROWS:]))
    first_a = collect(cut(collect(parts_a, LAST)), FIRST)
    last_a = collect(cut(collect(cut(group_a), FIRST)), DEPTH)
    first_a, last_a, returned_b = together(first_a, last_a, returned_b)

    parts_b = scatter_first(slots_b, returned_b[:ROWS], swap(returned_b[ROWS:]))
    group_b, parts_b = collect(cut(group_b), FIRST), collect(parts_b, LAST)
    last_b, first_b = collect(cut(group_b), DEPTH), collect(cut(parts_b), FIRST)
    return (
        jnp.concatenate([first_a, last_a], axis=1),
        jnp.concatenate([first_b, last_b], axis=1),
    )


def solution(mesh):
    in_specs = (
        P("section", "expert"),
        P("section", None),
        P("section", None),
        P("section", "expert"),
        P("section", None),
        P("section", None),
        P("section", "expert"),
        P("section", None, "expert"),
        P("section", None, "expert"),
        P("section", "expert", None),
    )
    out_specs = (P("section", "expert"), P("section", "expert"))
    return jax.shard_map(
        on_device, mesh=mesh, in_specs=in_specs, out_specs=out_specs, check_vma=False
    )
```

time: 421 us -> 379 us (0.900)
  blocking collectives: 81.1 us -> 0 us
  starting transfers between devices: 15.6 us -> 89.1 us
  Pallas kernels: 0 us -> 55 us
  matrix products: 39.8 us -> 0 us
  local copies, waits for them, and re-layouts: 63.9 us -> 27.8 us
  waiting for transfers between devices: 199 us -> 175 us
  other arithmetic: 3.37 us -> 10.3 us
    ppermute x0 -> x58, waiting for transfers between devices: none -> 175 us  [the longest x21 106 us: spread(): lax.ppermute(values, axis, shifts[4 - d])]
    reduce_scatter x2, waiting for transfers between devices: 91.8 us -> 0.02 us  [scatter_section(): lax.psum_scatter(dense, 'section', scatter_dimension=0, tiled=True, axis_...]
    ppermute x0 -> x58, starting transfers between devices: none -> 88.9 us  [the longest x30 58.3 us: collect(): arrived = [lax.ppermute(parts[d], axis, shifts[d]) for d in (1, 2, 3)]]
    all_gather x3 -> x2, waiting for transfers between devices: 88.9 us -> 0.03 us  [gather_section(): lax.all_gather(group, 'section', axis=0, tiled=True, axis_index_groups=LA...]
    all_to_all x3 -> x0, blocking collectives: 81.1 us -> none  [the longest x1 27.8 us: on_device(): lax.all_to_all(send_b, 'section', split_axis=0, concat_axis=0, tiled=True)]
    pallas_call x0 -> x9, Pallas kernels: none -> 55 us  [the longest x2 40.1 us: expert_call(): pl.pallas_call(backward_kernel if backward else forward_kernel, grid_spec...]
    dot_general x10 -> x0, matrix products: 39.8 us -> none  [the longest x2 12.4 us: on_device(): gate_out = jnp.dot(inputs, gate_cols, preferred_element_type=jnp.float32)]
    reshape x8 -> x0, local copies, waits for them, and re-layouts: 26.9 us -> none  [the longest x2 15.5 us: on_device(): inputs = whole_rows.reshape(sources * slots, width)]
  transfers between devices with their start and end apart: 7 -> 62, of which waited for: 6 -> 29; matrix products, arithmetic and copies ran while one was open for 21% -> 3% of each run, Pallas kernels for 0% -> 15%
where the time goes in v1:
time: 379 us; the launch traced here: 372 us
  waiting for transfers between devices  175 us (46%)
  starting transfers between devices  89.1 us (24%)
  Pallas kernels  55 us (15%)
  local copies, waits for them, and re-layouts  27.8 us (7%)
  between operations  15 us (4%)
  other arithmetic  10.3 us (3%)
    ppermute x21, waiting for transfers between devices, spread(): lax.ppermute(values, axis, shifts[4 - d])  106 us
    ppermute x30, starting transfers between devices, collect(): arrived = [lax.ppermute(parts[d], axis, shifts[d]) for d in (1, 2, 3)]  58.3 us
    ppermute x30, waiting for transfers between devices, collect(): arrived = [lax.ppermute(parts[d], axis, shifts[d]) for d in (1, 2, 3)]  56.3 us
    pallas_call x2, Pallas kernels, expert_call(): pl.pallas_call(backward_kernel if backward else forward_kernel, grid_spec...  40.1 us
    ppermute x21, starting transfers between devices, spread(): lax.ppermute(values, axis, shifts[4 - d])  29.4 us
    unnamed x81, local copies, waits for them, and re-layouts  22.7 us
    ppermute x7, waiting for transfers between devices, swap(): return lax.ppermute(values, 'section', SWAP)  11.9 us
  transfers between devices with their start and end apart: 62, of which 29 were waited for; matrix products, arithmetic and copies ran while one was open for 3% of the time, Pallas kernels for 15%

profile of v1, /device:TPU:16, one launch (start us, length us, event | category | flops | bytes accessed | tf_op | source)
XLA Modules:
  0.0 371.9 jit_solution(2169617826913417390)
XLA Ops:
  16.1 3.6 collective-permute-start.1
  20.6 4.1 %collective-permute-done.1 = bf16[64,1536]{1,0:T(8,128)(2,1)S(1)} collective-permute-done((bf16[64,1536]{1,0:T(8,128)(2,1)S(1)}, bf16[64,1536]{1,0:T(8,128)(2,1)S(1)}, u32[]{:S(2)}, u32[]{:S(2)}) %collective-permute-start.1) | collective-permute-done | bytes 196640 | tf_op jit(solution)/shard_map/ppermute | solution.py:64
  24.7 3.6 collective-permute-done
  35.3 7.5 %collective-permute-done.8 = bf16[256,512]{1,0:T(8,128)(2,1)S(1)} collective-permute-done((bf16[256,512]{1,0:T(8,128)(2,1)S(1)}, bf16[256,512]{1,0:T(8,128)(2,1)S(1)}, u32[]{:S(2)}, u32[]{:S(2)}) %collective-permute-start.8) | collective-permute-done | bytes 262176 | tf_op jit(solution)/shard_map/ppermute | solution.py:64
  43.1 5.2 %collective-permute-done.7 = bf16[256,512]{1,0:T(8,128)(2,1)S(1)} collective-permute-done((bf16[256,512]{1,0:T(8,128)(2,1)S(1)}, bf16[256,512]{1,0:T(8,128)(2,1)S(1)}, u32[]{:S(2)}, u32[]{:S(2)}) %collective-permute-start.7) | collective-permute-done | bytes 262176 | tf_op jit(solution)/shard_map/ppermute | solution.py:64
  48.3 3.8 %collective-permute-done.6 = bf16[256,512]{1,0:T(8,128)(2,1)S(1)} collective-permute-done((bf16[256,512]{1,0:T(8,128)(2,1)S(1)}, bf16[256,512]{1,0:T(8,128)(2,1)S(1)}, u32[]{:S(2)}, u32[]{:S(2)}) %collective-permute-start.6) | collective-permute-done | bytes 262176 | tf_op jit(solution)/shard_map/ppermute | solution.py:64
  52.1 5.1 %collective-permute-done.11.refs_3_ = bf16[256,1664]{1,0:T(8,128)(2,1)S(1)} collective-permute-done((bf16[256,1664]{1,0:T(8,128)(2,1)S(1)}, bf16[256,1664]{1,0:T(8,128)(2,1)S(1)}, u32[]{:S(2)}, u32[]{:S(2)}) %collective-permute-start.11) | collective-permute-done | bytes 852000 | tf_op jit(solution)/shard_map/ppermute | solution.py:64
  64.7 2.5 shard_map.113
  80.4 13.0 %collective-permute-done.17 = bf16[256,1024]{1,0:T(8,128)(2,1)S(1)} collective-permute-done((bf16[256,1024]{1,0:T(8,128)(2,1)S(1)}, bf16[256,1024]{1,0:T(8,128)(2,1)S(1)}, u32[]{:S(2)}, u32[]{:S(2)}) %collective-permute-start.17) | collective-permute-done | bytes 524320 | tf_op jit(solution)/shard_map/ppermute | solution.py:64
  93.4 11.0 %collective-permute-done.16 = bf16[256,1024]{1,0:T(8,128)(2,1)S(1)} collective-permute-done((bf16[256,1024]{1,0:T(8,128)(2,1)S(1)}, bf16[256,1024]{1,0:T(8,128)(2,1)S(1)}, u32[]{:S(2)}, u32[]{:S(2)}) %collective-permute-start.16) | collective-permute-done | bytes 524320 | tf_op jit(solution)/shard_map/ppermute | solution.py:64
  113.2 2.9 collective-permute-done.22.refs_5_
  116.1 15.5 %shard_map.115 = (bf16[640,512]{1,0:T(8,128)(2,1)S(1)}, bf16[640,512]{1,0:T(8,128)(2,1)S(1)}, bf16[640,512]{1,0:T(8,128)(2,1)S(1)}, bf16[640,512]{1,0:T(8,128)(2...) custom-call(s32[4]{0:T(128)S(1)} %pad_add_fusion.where, bf16[640,512]{1,0:T(8,128)(2,1)S(1)} %copy-done.6, ...), custom_call_target="tpu_custom_call" | custom-call | flops 125829120 | bytes 491520 | tf_op jit(solution)/shard_map/pallas_call | solution.py:337
  141.4 52.6 %collective-permute-done.15.refs_3_ = bf16[640,1024]{1,0:T(8,128)(2,1)} collective-permute-done((bf16[640,1024]{1,0:T(8,128)(2,1)}, bf16[640,1024]{1,0:T(8,128)(2,1)}, u32[]{:S(2)}, u32[]{:S(2)}) %collective-permute-start.15) | collective-permute-done | bytes 1310752 | tf_op jit(solution)/shard_map/ppermute | solution.py:64
  194.7 3.4 copy-done.3
  198.1 4.5 %shard_map.117 = (bf16[320,4096]{1,0:T(8,128)(2,1)S(1)}, bf16[320,4096]{1,0:T(8,128)(2,1)S(1)}) custom-call(s32[4]{0:T(128)S(1)} %pad_add_fusion.where, bf16[4,160,256]{2,1,0:T(8,128)(2,1)S(1)} %get-tuple-element.77.slots_ref, bf16[4096,1024]{1,0:T(8,128)(2,1)S(1)} %copy-done.3), custom_call_target="tpu_custom_call" | custom-call | flops 20971520 | bytes 458752 | tf_op jit(solution)/shard_map/pallas_call | solution.py:173
  204.3 4.9 %collective-permute-done.24.refs_5_ = bf16[320,4096]{1,0:T(8,128)(2,1)S(1)} collective-permute-done((bf16[320,4096]{1,0:T(8,128)(2,1)S(1)}, bf16[320,4096]{1,0:T(8,128)(2,1)S(1)}, u32[]{:S(2)}, u32[]{:S(2)}) %collective-permute-start.24) | collective-permute-done | bytes 2621472 | tf_op jit(solution)/shard_map/ppermute | solution.py:77
  210.7 24.6 %shard_map.118 = (bf16[640,512]{1,0:T(8,128)(2,1)S(1)}, bf16[640,512]{1,0:T(8,128)(2,1)S(1)}, bf16[640,512]{1,0:T(8,128)(2,1)S(1)}, bf16[640,512]{1,0:T(8,128)(2...) custom-call(s32[4]{0:T(128)S(1)} %pad_add_fusion.where, ...), custom_call_target="tpu_custom_call" | custom-call | flops 209715200 | bytes 491520 | tf_op jit(solution)/shard_map/pallas_call | solution.py:337
  235.8 3.5 collective-permute-start.27
  239.4 14.4 %collective-permute-done.26 = bf16[640,512]{1,0:T(8,128)(2,1)S(1)} collective-permute-done((bf16[640,512]{1,0:T(8,128)(2,1)S(1)}, bf16[640,512]{1,0:T(8,128)(2,1)S(1)}, u32[]{:S(2)}, u32[]{:S(2)}) %collective-permute-start.26) | collective-permute-done | bytes 655392 | tf_op jit(solution)/shard_map/ppermute | solution.py:69
  253.8 14.6 %collective-permute-done.27 = bf16[640,512]{1,0:T(8,128)(2,1)S(1)} collective-permute-done((bf16[640,512]{1,0:T(8,128)(2,1)S(1)}, bf16[640,512]{1,0:T(8,128)(2,1)S(1)}, u32[]{:S(2)}, u32[]{:S(2)}) %collective-permute-start.27) | collective-permute-done | bytes 655392 | tf_op jit(solution)/shard_map/ppermute | solution.py:69
  286.8 3.6 collective-permute-start.30
  290.6 3.2 collective-permute-start.41
  305.1 2.6 collective-permute-done.32
  310.0 6.4 %collective-permute-done.42 = bf16[640,512]{1,0:T(8,128)(2,1)S(1)} collective-permute-done((bf16[640,512]{1,0:T(8,128)(2,1)S(1)}, bf16[640,512]{1,0:T(8,128)(2,1)S(1)}, u32[]{:S(2)}, u32[]{:S(2)}) %collective-permute-start.42) | collective-permute-done | bytes 655392 | tf_op jit(solution)/shard_map/ppermute | solution.py:69
  316.4 11.8 %collective-permute-start.34 = (bf16[64,512]{1,0:T(8,128)(2,1)S(1)}, bf16[64,512]{1,0:T(8,128)(2,1)S(1)}, u32[]{:S(2)}, u32[]{:S(2)}) collective-permute-start(bf16[64,512]{1,0:T(8,128)(2,1)S(1)} %get-tuple-element.147), channel_id=1, source_target_pairs={{0,64},{4,20},{8,72},{12,28},{16,80},{20,4},{24,88},{28,12},{32,96... | collective-permute-start | bytes 196616 | tf_op jit(solution)/shard_map/ppermute | solution.py:69
  334.0 2.6 collective-permute-start.47
  339.0 2.6 collective-permute-start.52
  341.6 4.2 %collective-permute-start.53 = (bf16[256,512]{1,0:T(8,128)(2,1)S(1)}, bf16[256,512]{1,0:T(8,128)(2,1)S(1)}, u32[]{:S(2)}, u32[]{:S(2)}) collective-permute-start(bf16[256,512]{1,0:T(8,128)(2,1)S(1)} %get-tuple-element.128), channel_id=1, source_target_pairs={{0,64},{4,20},{8,72},{12,28},{16,80},{20,4},{24,88},{28,12},{32,96... | collective-permute-start | bytes 786440 | tf_op jit(solution)/shard_map/ppermute | solution.py:69
  346.0 3.4 collective-permute-start.49
  349.5 4.6 %collective-permute-start.50 = (bf16[64,512]{1,0:T(8,128)(2,1)S(1)}, bf16[64,512]{1,0:T(8,128)(2,1)S(1)}, u32[]{:S(2)}, u32[]{:S(2)}) collective-permute-start(bf16[64,512]{1,0:T(8,128)(2,1)S(1)} %get-tuple-element.138), channel_id=1, source_target_pairs={{0,64},{4,20},{8,72},{12,28},{16,80},{20,4},{24,88},{28,12},{32,96... | collective-permute-start | bytes 196616 | tf_op jit(solution)/shard_map/ppermute | solution.py:69
  355.3 3.2 collective-permute-start.57
  361.0 3.3 collective-permute-done.56
  (239 shorter events, 105.1 us)
Async XLA Ops:
  7.2 101.4 %all-gather.3.cloned.1.call-start = ((), (), s32[]{:S(2)}) async-start(), calls=%async_computation.2 | async-start | bytes 5242880 | tf_op jit(solution)/shard_map/all_gather | solution.py:379
  13.0 15.3 %collective-permute-start.5 = (bf16[64,1664]{1,0:T(8,128)(2,1)S(1)}, bf16[64,1664]{1,0:T(8,128)(2,1)S(1)}, u32[]{:S(2)}, u32[]{:S(2)}) collective-permute-start(bf16[64,1664]{1,0:T(8,128)(2,1)S(1)} %concatenate.34), channel_id=1, source_target_pairs={{0,32},{4,12},{8,40},{12,20},{16,48},{20,28},{24,56},{28,4},{32,64... | collective-permute-start | bytes 638984 | tf_op jit(solution)/shard_map/ppermute | solution.py:64
  14.4 14.0 %collective-permute-start.4 = (bf16[64,1664]{1,0:T(8,128)(2,1)S(1)}, bf16[64,1664]{1,0:T(8,128)(2,1)S(1)}, u32[]{:S(2)}, u32[]{:S(2)}) collective-permute-start(bf16[64,1664]{1,0:T(8,128)(2,1)S(1)} %concatenate.34), channel_id=1, source_target_pairs={{0,64},{4,20},{8,72},{12,28},{16,80},{20,4},{24,88},{28,12},{32,96... | collective-permute-start | bytes 638984 | tf_op jit(solution)/shard_map/ppermute | solution.py:64
  15.0 13.4 %collective-permute-start.3 = (bf16[64,1664]{1,0:T(8,128)(2,1)S(1)}, bf16[64,1664]{1,0:T(8,128)(2,1)S(1)}, u32[]{:S(2)}, u32[]{:S(2)}) collective-permute-start(bf16[64,1664]{1,0:T(8,128)(2,1)S(1)} %concatenate.34), channel_id=1, source_target_pairs={{0,96},{4,28},{8,104},{12,4},{16,112},{20,12},{24,120},{28,20},{32... | collective-permute-start | bytes 638984 | tf_op jit(solution)/shard_map/ppermute | solution.py:64
  28.5 28.7 %collective-permute-start.11 = (bf16[256,1664]{1,0:T(8,128)(2,1)S(1)}, bf16[256,1664]{1,0:T(8,128)(2,1)S(1)}, u32[]{:S(2)}, u32[]{:S(2)}) collective-permute-start(bf16[256,1664]{1,0:T(8,128)(2,1)S(1)} %constant_dynamic-update-slice_fusion.refs_0_), channel_id=1, source_target_pairs={{0,8},{4,36},{8,16},{12,44},{16,24},{20,52},{24,0},{28,60},{32,40}... | collective-permute-start | bytes 2555912 | tf_op jit(solution)/shard_map/ppermute | solution.py:64
  30.6 27.5 %collective-permute-start.10 = (bf16[256,1664]{1,0:T(8,128)(2,1)S(1)}, bf16[256,1664]{1,0:T(8,128)(2,1)S(1)}, u32[]{:S(2)}, u32[]{:S(2)}) collective-permute-start(bf16[256,1664]{1,0:T(8,128)(2,1)S(1)} %constant_dynamic-update-slice_fusion.refs_0_), channel_id=1, source_target_pairs={{0,16},{4,68},{8,24},{12,76},{16,0},{20,84},{24,8},{28,92},{32,48}... | collective-permute-start | bytes 2555912 | tf_op jit(solution)/shard_map/ppermute | solution.py:64
  31.7 27.4 %collective-permute-start.9 = (bf16[256,1664]{1,0:T(8,128)(2,1)S(1)}, bf16[256,1664]{1,0:T(8,128)(2,1)S(1)}, u32[]{:S(2)}, u32[]{:S(2)}) collective-permute-start(bf16[256,1664]{1,0:T(8,128)(2,1)S(1)} %constant_dynamic-update-slice_fusion.refs_0_), channel_id=1, source_target_pairs={{0,24},{4,100},{8,0},{12,108},{16,8},{20,116},{24,16},{28,124},{32... | collective-permute-start | bytes 2555912 | tf_op jit(solution)/shard_map/ppermute | solution.py:64
  34.8 13.5 %collective-permute-start.7 = (bf16[256,512]{1,0:T(8,128)(2,1)S(1)}, bf16[256,512]{1,0:T(8,128)(2,1)S(1)}, u32[]{:S(2)}, u32[]{:S(2)}) collective-permute-start(bf16[256,512]{1,0:T(8,128)(2,1)S(1)} %pad_maximum_fusion.5), channel_id=1, source_target_pairs={{0,64},{4,20},{8,72},{12,28},{16,80},{20,4},{24,88},{28,12},{32,96... | collective-permute-start | bytes 786440 | tf_op jit(solution)/shard_map/ppermute | solution.py:64
  61.0 133.7 %all-gather.5.cloned.1.call-start = ((), (), s32[]{:S(2)}) async-start(), calls=%async_computation.3 | async-start | bytes 10485760 | tf_op jit(solution)/shard_map/all_gather | solution.py:379
  70.2 34.3 %collective-permute-start.21 = (bf16[640,512]{1,0:T(8,128)(2,1)S(1)}, bf16[640,512]{1,0:T(8,128)(2,1)S(1)}, u32[]{:S(2)}, u32[]{:S(2)}) collective-permute-start(bf16[640,512]{1,0:T(8,128)(2,1)S(1)} %pad_maximum_fusion.3.refs_0_), channel_id=1, source_target_pairs={{0,1},{1,2},{2,3},{3,0},{4,5},{5,6},{6,7},{7,4},{8,9},{9,10},{10,1... | collective-permute-start | bytes 1966088 | tf_op jit(solution)/shard_map/ppermute | solution.py:64
  72.6 32.7 %collective-permute-start.20 = (bf16[640,512]{1,0:T(8,128)(2,1)S(1)}, bf16[640,512]{1,0:T(8,128)(2,1)S(1)}, u32[]{:S(2)}, u32[]{:S(2)}) collective-permute-start(bf16[640,512]{1,0:T(8,128)(2,1)S(1)} %pad_maximum_fusion.3.refs_0_), channel_id=1, source_target_pairs={{0,2},{1,3},{2,0},{3,1},{4,6},{5,7},{6,4},{7,5},{8,10},{9,11},{10,... | collective-permute-start | bytes 1966088 | tf_op jit(solution)/shard_map/ppermute | solution.py:64
  75.0 31.1 %collective-permute-start.19 = (bf16[640,512]{1,0:T(8,128)(2,1)S(1)}, bf16[640,512]{1,0:T(8,128)(2,1)S(1)}, u32[]{:S(2)}, u32[]{:S(2)}) collective-permute-start(bf16[640,512]{1,0:T(8,128)(2,1)S(1)} %pad_maximum_fusion.3.refs_0_), channel_id=1, source_target_pairs={{0,3},{1,0},{2,1},{3,2},{4,7},{5,4},{6,5},{7,6},{8,11},{9,8},{10,9... | collective-permute-start | bytes 1966088 | tf_op jit(solution)/shard_map/ppermute | solution.py:64
  77.2 16.3 %collective-permute-start.17 = (bf16[256,1024]{1,0:T(8,128)(2,1)S(1)}, bf16[256,1024]{1,0:T(8,128)(2,1)S(1)}, u32[]{:S(2)}, u32[]{:S(2)}) collective-permute-start(bf16[256,1024]{1,0:T(8,128)(2,1)S(1)} %pad_maximum_fusion.4), channel_id=1, source_target_pairs={{0,64},{4,20},{8,72},{12,28},{16,80},{20,4},{24,88},{28,12},{32,96... | collective-permute-start | bytes 1572872 | tf_op jit(solution)/shard_map/ppermute | solution.py:64
  78.3 26.2 %collective-permute-start.16 = (bf16[256,1024]{1,0:T(8,128)(2,1)S(1)}, bf16[256,1024]{1,0:T(8,128)(2,1)S(1)}, u32[]{:S(2)}, u32[]{:S(2)}) collective-permute-start(bf16[256,1024]{1,0:T(8,128)(2,1)S(1)} %pad_maximum_fusion.4), channel_id=1, source_target_pairs={{0,96},{4,28},{8,104},{12,4},{16,112},{20,12},{24,120},{28,20},{32... | collective-permute-start | bytes 1572872 | tf_op jit(solution)/shard_map/ppermute | solution.py:64
  108.5 164.9 %reduce-scatter.3.cloned.1.call-start = ((), (), s32[]{:S(2)}) async-start(), calls=%async_computation.4 | async-start | bytes 5242880 | tf_op jit(solution)/shard_map/reduce_scatter | solution.py:384
  133.6 60.4 %collective-permute-start.15 = (bf16[640,1024]{1,0:T(8,128)(2,1)}, bf16[640,1024]{1,0:T(8,128)(2,1)}, u32[]{:S(2)}, u32[]{:S(2)}) collective-permute-start(bf16[640,1024]{1,0:T(8,128)(2,1)} %pad_maximum_fusion.1.refs_0_), channel_id=1, source_target_pairs={{0,1},{1,2},{2,3},{3,0},{4,5},{5,6},{6,7},{7,4},{8,9},{9,10},{10,1... | collective-permute-start | bytes 3932168 | tf_op jit(solution)/shard_map/ppermute | solution.py:64
  133.8 60.2 %collective-permute-start.14 = (bf16[640,1024]{1,0:T(8,128)(2,1)}, bf16[640,1024]{1,0:T(8,128)(2,1)}, u32[]{:S(2)}, u32[]{:S(2)}) collective-permute-start(bf16[640,1024]{1,0:T(8,128)(2,1)} %pad_maximum_fusion.1.refs_0_), channel_id=1, source_target_pairs={{0,2},{1,3},{2,0},{3,1},{4,6},{5,7},{6,4},{7,5},{8,10},{9,11},{10,... | collective-permute-start | bytes 3932168 | tf_op jit(solution)/shard_map/ppermute | solution.py:64
  135.2 59.4 %collective-permute-start.13 = (bf16[640,1024]{1,0:T(8,128)(2,1)}, bf16[640,1024]{1,0:T(8,128)(2,1)}, u32[]{:S(2)}, u32[]{:S(2)}) collective-permute-start(bf16[640,1024]{1,0:T(8,128)(2,1)} %pad_maximum_fusion.1.refs_0_), channel_id=1, source_target_pairs={{0,3},{1,0},{2,1},{3,2},{4,7},{5,4},{6,5},{7,6},{8,11},{9,8},{10,9... | collective-permute-start | bytes 3932168 | tf_op jit(solution)/shard_map/ppermute | solution.py:64
  194.6 143.2 %reduce-scatter.5.cloned.1.call-start = ((), (), s32[]{:S(2)}) async-start(), calls=%async_computation.5 | async-start | bytes 5242880 | tf_op jit(solution)/shard_map/reduce_scatter | solution.py:384
  235.3 33.5 %collective-permute-start.25 = (bf16[320,2048]{1,0:T(8,128)(2,1)S(1)}, bf16[320,2048]{1,0:T(8,128)(2,1)S(1)}, u32[]{:S(2)}, u32[]{:S(2)}) collective-permute-start(bf16[320,2048]{1,0:T(8,128)(2,1)S(1)} %get-tuple-element.103), channel_id=1, source_target_pairs={{0,4},{4,0},{8,12},{12,8},{16,20},{20,16},{24,28},{28,24},{32,36},... | collective-permute-start | bytes 3932168 | tf_op jit(solution)/shard_map/ppermute | solution.py:77
  235.5 18.2 %collective-permute-start.26 = (bf16[640,512]{1,0:T(8,128)(2,1)S(1)}, bf16[640,512]{1,0:T(8,128)(2,1)S(1)}, u32[]{:S(2)}, u32[]{:S(2)}) collective-permute-start(bf16[640,512]{1,0:T(8,128)(2,1)S(1)} %copy-done.35), channel_id=1, source_target_pairs={{0,1},{1,2},{2,3},{3,0},{4,5},{5,6},{6,7},{7,4},{8,9},{9,10},{10,1... | collective-permute-start | bytes 1966088 | tf_op jit(solution)/shard_map/ppermute | solution.py:69
  235.8 32.5 %collective-permute-start.27 = (bf16[640,512]{1,0:T(8,128)(2,1)S(1)}, bf16[640,512]{1,0:T(8,128)(2,1)S(1)}, u32[]{:S(2)}, u32[]{:S(2)}) collective-permute-start(bf16[640,512]{1,0:T(8,128)(2,1)S(1)} %copy-done.33), channel_id=1, source_target_pairs={{0,2},{1,3},{2,0},{3,1},{4,6},{5,7},{6,4},{7,5},{8,10},{9,11},{10,... | collective-permute-start | bytes 1966088 | tf_op jit(solution)/shard_map/ppermute | solution.py:69
  239.4 29.1 %collective-permute-start.28 = (bf16[640,512]{1,0:T(8,128)(2,1)S(1)}, bf16[640,512]{1,0:T(8,128)(2,1)S(1)}, u32[]{:S(2)}, u32[]{:S(2)}) collective-permute-start(bf16[640,512]{1,0:T(8,128)(2,1)S(1)} %copy-done.31), channel_id=1, source_target_pairs={{0,3},{1,0},{2,1},{3,2},{4,7},{5,4},{6,5},{7,6},{8,11},{9,8},{10,9... | collective-permute-start | bytes 1966088 | tf_op jit(solution)/shard_map/ppermute | solution.py:69
  286.8 14.0 %collective-permute-start.30 = (bf16[256,512]{1,0:T(8,128)(2,1)S(1)}, bf16[256,512]{1,0:T(8,128)(2,1)S(1)}, u32[]{:S(2)}, u32[]{:S(2)}) collective-permute-start(bf16[256,512]{1,0:T(8,128)(2,1)S(1)} %get-tuple-element.110), channel_id=1, source_target_pairs={{0,8},{4,36},{8,16},{12,44},{16,24},{20,52},{24,0},{28,60},{32,40}... | collective-permute-start | bytes 786440 | tf_op jit(solution)/shard_map/ppermute | solution.py:69
  297.2 19.1 %collective-permute-start.42 = (bf16[640,512]{1,0:T(8,128)(2,1)S(1)}, bf16[640,512]{1,0:T(8,128)(2,1)S(1)}, u32[]{:S(2)}, u32[]{:S(2)}) collective-permute-start(bf16[640,512]{1,0:T(8,128)(2,1)S(1)} %copy-done.29), channel_id=1, source_target_pairs={{0,1},{1,2},{2,3},{3,0},{4,5},{5,6},{6,7},{7,4},{8,9},{9,10},{10,1... | collective-permute-start | bytes 1966088 | tf_op jit(solution)/shard_map/ppermute | solution.py:69
  300.3 27.9 %collective-permute-start.43 = (bf16[640,512]{1,0:T(8,128)(2,1)S(1)}, bf16[640,512]{1,0:T(8,128)(2,1)S(1)}, u32[]{:S(2)}, u32[]{:S(2)}) collective-permute-start(bf16[640,512]{1,0:T(8,128)(2,1)S(1)} %copy-done.27), channel_id=1, source_target_pairs={{0,2},{1,3},{2,0},{3,1},{4,6},{5,7},{6,4},{7,5},{8,10},{9,11},{10,... | collective-permute-start | bytes 1966088 | tf_op jit(solution)/shard_map/ppermute | solution.py:69
  300.8 27.4 %collective-permute-start.44 = (bf16[640,512]{1,0:T(8,128)(2,1)S(1)}, bf16[640,512]{1,0:T(8,128)(2,1)S(1)}, u32[]{:S(2)}, u32[]{:S(2)}) collective-permute-start(bf16[640,512]{1,0:T(8,128)(2,1)S(1)} %copy-done.25), channel_id=1, source_target_pairs={{0,3},{1,0},{2,1},{3,2},{4,7},{5,4},{6,5},{7,6},{8,11},{9,8},{10,9... | collective-permute-start | bytes 1966088 | tf_op jit(solution)/shard_map/ppermute | solution.py:69
  307.9 20.7 %collective-permute-start.33 = (bf16[64,512]{1,0:T(8,128)(2,1)S(1)}, bf16[64,512]{1,0:T(8,128)(2,1)S(1)}, u32[]{:S(2)}, u32[]{:S(2)}) collective-permute-start(bf16[64,512]{1,0:T(8,128)(2,1)S(1)} %get-tuple-element.145), channel_id=1, source_target_pairs={{0,32},{4,12},{8,40},{12,20},{16,48},{20,28},{24,56},{28,4},{32,64... | collective-permute-start | bytes 196616 | tf_op jit(solution)/shard_map/ppermute | solution.py:69
  309.5 19.1 %collective-permute-start.35 = (bf16[64,512]{1,0:T(8,128)(2,1)S(1)}, bf16[64,512]{1,0:T(8,128)(2,1)S(1)}, u32[]{:S(2)}, u32[]{:S(2)}) collective-permute-start(bf16[64,512]{1,0:T(8,128)(2,1)S(1)} %get-tuple-element.146), channel_id=1, source_target_pairs={{0,96},{4,28},{8,104},{12,4},{16,112},{20,12},{24,120},{28,20},{32... | collective-permute-start | bytes 196616 | tf_op jit(solution)/shard_map/ppermute | solution.py:69
  316.4 14.1 %collective-permute-start.34 = (bf16[64,512]{1,0:T(8,128)(2,1)S(1)}, bf16[64,512]{1,0:T(8,128)(2,1)S(1)}, u32[]{:S(2)}, u32[]{:S(2)}) collective-permute-start(bf16[64,512]{1,0:T(8,128)(2,1)S(1)} %get-tuple-element.147), channel_id=1, source_target_pairs={{0,64},{4,20},{8,72},{12,28},{16,80},{20,4},{24,88},{28,12},{32,96... | collective-permute-start | bytes 196616 | tf_op jit(solution)/shard_map/ppermute | solution.py:69
  341.6 12.4 %collective-permute-start.54 = (bf16[256,512]{1,0:T(8,128)(2,1)S(1)}, bf16[256,512]{1,0:T(8,128)(2,1)S(1)}, u32[]{:S(2)}, u32[]{:S(2)}) collective-permute-start(bf16[256,512]{1,0:T(8,128)(2,1)S(1)} %get-tuple-element.127), channel_id=1, source_target_pairs={{0,96},{4,28},{8,104},{12,4},{16,112},{20,12},{24,120},{28,20},{32... | collective-permute-start | bytes 786440 | tf_op jit(solution)/shard_map/ppermute | solution.py:69
  346.0 12.5 %collective-permute-start.49 = (bf16[64,512]{1,0:T(8,128)(2,1)S(1)}, bf16[64,512]{1,0:T(8,128)(2,1)S(1)}, u32[]{:S(2)}, u32[]{:S(2)}) collective-permute-start(bf16[64,512]{1,0:T(8,128)(2,1)S(1)} %get-tuple-element.136), channel_id=1, source_target_pairs={{0,32},{4,12},{8,40},{12,20},{16,48},{20,28},{24,56},{28,4},{32,64... | collective-permute-start | bytes 196616 | tf_op jit(solution)/shard_map/ppermute | solution.py:69
  (69 other events, 665.7 us)
Sparse Core Ops, SparseCore 0:
  61.1 45.4 all-gather.2
  108.6 50.4 all-gather.4
  194.8 31.1 reduce-scatter.2
  273.5 36.9 reduce-scatter.4

commit v2 on v1

--- a/solution.py
+++ b/solution.py
@@ -64,13 +64,28 @@
     return [values] + [lax.ppermute(values, axis, shifts[4 - d]) for d in (1, 2, 3)]
 
 
-def collect(parts, ring):
+DEPTH_RING = [
+    (s * 4 + z, s * 4 + (z + (1 if s % CORES == 0 else 3)) % 4) for s in range(32) for z in range(4)
+]
+
+
+def around(values, steps):
+    parts = [values]
+    for _ in range(steps):
+        parts.append(lax.ppermute(parts[-1], ("section", "expert"), DEPTH_RING))
+    return parts
+
+
+def send(parts, ring):
     axis, shifts = ring
-    arrived = [lax.ppermute(parts[d], axis, shifts[d]) for d in (1, 2, 3)]
-    total = parts[0].astype(F32)
-    for part in arrived:
-        total = total + part.astype(F32)
-    return total.astype(BF16)
+    return [parts[0]] + [lax.ppermute(parts[d], axis, shifts[d]) for d in (1, 2, 3)]
+
+
+def total(parts):
+    value = parts[0].astype(F32)
+    for part in parts[1:]:
+        value = value + part.astype(F32)
+    return value.astype(BF16)
 
 
 def swap(values):
@@ -151,8 +166,13 @@
     )(where, *parts)
 
 
-def along(where, distance, width):
+def along(where, distance, width, size=HALF):
     start = lax.rem(where[0] + distance, 4) * width
+    return pl.ds(pl.multiple_of(start, HALF), size)
+
+
+def turned(where, number, width):
+    start = lax.rem(where[0] + number * where[4], 4) * width
     return pl.ds(pl.multiple_of(start, HALF), HALF)
 
 
@@ -210,7 +230,8 @@
 
 def scatter_last_kernel(where, slots_ref, own_ref, sibling_ref, out_ref):
     for z in range(4):
-        columns = along(where, z, HALF)
+        width = out_ref.shape[1]
+        columns = along(where, z, width, width)
         rows = jnp.concatenate([own_ref[:, columns], sibling_ref[:, columns]], axis=0)
         dense = dot_first(slots_ref[0], rows).astype(BF16)
         for part in range(4):
@@ -218,42 +239,85 @@
 
 
 def scatter_last(where, slots, own, sibling):
+    width = own.shape[1] // 4
     return pl.pallas_call(
         scatter_last_kernel,
         grid_spec=pltpu.PrefetchScalarGridSpec(
             num_scalar_prefetch=1,
             grid=(4,),
             in_specs=[pl.BlockSpec((1, 2 * SLOTS, GROUP), lambda i, w: (i, 0, 0))]
-            + [pl.BlockSpec((SLOTS, 4 * HALF), lambda i, w: (i, 0))] * 2,
-            out_specs=pl.BlockSpec((4 * GROUP, HALF), lambda i, w: (lax.rem(w[3] + i, 4), 0)),
+            + [pl.BlockSpec((SLOTS, 4 * width), lambda i, w: (i, 0))] * 2,
+            out_specs=pl.BlockSpec((4 * GROUP, width), lambda i, w: (lax.rem(w[3] + i, 4), 0)),
         ),
-        out_shape=jax.ShapeDtypeStruct((16 * GROUP, HALF), BF16),
+        out_shape=jax.ShapeDtypeStruct((16 * GROUP, width), BF16),
         compiler_params=params(16),
-        cost_estimate=cost(2 * 16 * 2 * SLOTS * GROUP * HALF, 14 * 2**20),
+        cost_estimate=cost(2 * 16 * 2 * SLOTS * GROUP * width, 28 * 2**20),
     )(where, slots, own, sibling)
 
 
-def lay_out(where, near, last, out_ref):
+def feature_copies(where, near, last, target, sems, part, first_near, first_last, spot):
+    copies = []
     for z in range(4):
-        out_ref[:, along(where, z, 2 * HALF)] = near[z]
-        out_ref[:, (2 * z + 1) * HALF : (2 * z + 2) * HALF] = last[z]
-
-
-def halves(ref, first=0):
-    return [ref[:, first + z * HALF : first + (z + 1) * HALF] for z in range(4)]
-
-
-def write_result(where, weight, product, near_out, last_out):
-    step = pl.program_id(0)
+        copies.append(
+            pltpu.make_async_copy(
+                near[z].at[pl.ds(part * ROWS, ROWS), pl.ds(first_near, HALF)],
+                target.at[part, :, spot(where, z, 2 * HALF)],
+                sems.at[part, 2 * z],
+            )
+        )
+        copies.append(
+            pltpu.make_async_copy(
+                last[part].at[:, pl.ds(first_last + z * HALF, HALF)],
+                target.at[part, :, pl.ds((2 * z + 1) * HALF, HALF)],
+                sems.at[part, 2 * z + 1],
+            )
+        )
+    return copies
+
+
+def wait_part(copies):
+    for part in range(2):
+
+        @pl.when(pl.program_id(0) == part)
+        def _():
+            for copy in copies[part]:
+                copy.wait()
+
+
+def wait_first(copy):
+    @pl.when(pl.program_id(0) == 0)
+    def _():
+        copy.wait()
+
+
+def start_first(copies):
+    @pl.when(pl.program_id(0) == 0)
+    def _():
+        for copy in copies:
+            copy.start()
+
+
+def write_result(weight, product, outs):
+    for block in range(8):
+        columns = slice(block * HALF, (block + 1) * HALF)
+        value = (product(columns) * weight).astype(BF16)
+        for part in range(2):
+
+            @pl.when(pl.program_id(0) == part)
+            def _():
+                outs[part][:, columns] = value
+
+
+def write_halves(where, weight, product, near, last):
     for z in range(4):
-        near_out[z][...] = (product(along(where, z, 2 * HALF)) * weight).astype(BF16)
+        near[z][...] = (product(along(where, z, 2 * HALF)) * weight).astype(BF16)
     for z in range(4):
         value = (product(pl.ds((2 * z + 1) * HALF, HALF)) * weight).astype(BF16)
         for part in range(2):
 
-            @pl.when(step == part)
+            @pl.when(pl.program_id(0) == part)
             def _():
-                last_out[part][:, z * HALF : (z + 1) * HALF] = value
+                last[part][:, z * HALF : (z + 1) * HALF] = value
 
 
 def pick(refs):
@@ -267,89 +331,101 @@
 
 
 def forward_kernel(where, *refs):
-    near, last, metas, (gate_ref, up_ref, down_ref) = refs[:4], refs[4:6], refs[6:8], refs[8:11]
-    near_out, last_out, (values, hidden) = refs[11:15], refs[15:17], refs[17:]
-    near = [r[...] for r in near]
-    for part in range(2):
-
-        @pl.when(pl.program_id(0) == part)
-        def _():
-            lay_out(where, near, halves(last[part]), values)
-
-    gate = dot(values[...], gate_ref[0])
-    upward = dot(values[...], up_ref[0])
+    near, last, metas, weights = refs[:4], refs[4:6], refs[6:8], refs[8:11]
+    outs = refs[11:13]
+    gate_ref, up_ref, down_ref, weight_sems, values, sems, hidden = refs[13:]
+    step = pl.program_id(0)
+    rows = [feature_copies(where, near, last, values, sems, p, 0, 0, along) for p in range(2)]
+    held = (gate_ref, up_ref, down_ref)
+    matrices = [pltpu.make_async_copy(weights[n], held[n], weight_sems.at[n]) for n in range(3)]
+    start_first(rows[0] + matrices + rows[1])
+    weight = slot_weight(pick(metas), BASES[0], where[1])
+    wait_part(rows)
+    wait_first(matrices[0])
+    gate = dot(values[step], gate_ref[0])
+    wait_first(matrices[1])
+    upward = dot(values[step], up_ref[0])
     hidden[...] = (gate / (1.0 + jnp.exp(-gate)) * upward).astype(BF16)
-    weight = slot_weight(pick(metas), BASES[0], where[1])
+    wait_first(matrices[2])
 
     def product(columns):
         return dot(hidden[...], down_ref[0, :, columns])
 
-    write_result(where, weight, product, near_out, last_out)
+    write_result(weight, product, outs)
 
 
 def backward_kernel(where, *refs):
-    near, last, metas, (gate_ref, up_ref, down_ref) = refs[:4], refs[4:6], refs[6:8], refs[8:11]
-    near_out, last_out, (values, cotangent, gate_grad, up_grad) = refs[11:15], refs[15:17], refs[17:]
-    for part in range(2):
-
-        @pl.when(pl.program_id(0) == part)
-        def _():
-            lay_out(where, [r[:, :HALF] for r in near], halves(last[part]), values)
-            lay_out(where, [r[:, HALF:] for r in near], halves(last[part], 4 * HALF), cotangent)
-
-    gate = dot(values[...], gate_ref[0])
-    upward = dot(values[...], up_ref[0])
-    grad = dot_last(cotangent[...], down_ref[0])
+    near, last, metas, weights = refs[:4], refs[4:6], refs[6:8], refs[8:11]
+    near_out, last_out = refs[11:15], refs[15:17]
+    gate_ref, up_ref, down_ref, weight_sems, values, sems = refs[17:23]
+    cotangent, cot_sems, gate_grad, up_grad = refs[23:]
+    step = pl.program_id(0)
+    rows = [feature_copies(where, near, last, values, sems, p, 0, 0, turned) for p in range(2)]
+    cots = [
+        feature_copies(where, near, last, cotangent, cot_sems, p, HALF, 4 * HALF, turned)
+        for p in range(2)
+    ]
+    held = (gate_ref, up_ref, down_ref)
+    matrices = [pltpu.make_async_copy(weights[n], held[n], weight_sems.at[n]) for n in range(3)]
+    start_first(rows[0] + matrices[:2] + cots[0] + matrices[2:] + rows[1] + cots[1])
+    weight = slot_weight(pick(metas), BASES[1], where[1])
+    wait_part(rows)
+    wait_first(matrices[0])
+    gate = dot(values[step], gate_ref[0])
+    wait_first(matrices[1])
+    upward = dot(values[step], up_ref[0])
+    wait_part(cots)
+    wait_first(matrices[2])
+    grad = dot_last(cotangent[step], down_ref[0])
     sigmoid = 1.0 / (1.0 + jnp.exp(-gate))
     scaled = grad * sigmoid
     gate_grad[...] = (scaled * upward * (1.0 + gate * (1.0 - sigmoid))).astype(BF16)
     up_grad[...] = (scaled * gate).astype(BF16)
-    weight = slot_weight(pick(metas), BASES[1], where[1])
 
     def product(rows):
         return dot_last(gate_grad[...], gate_ref[0, rows]) + dot_last(up_grad[...], up_ref[0, rows])
 
-    write_result(where, weight, product, near_out, last_out)
+    write_halves(where, weight, product, near_out, last_out)
 
 
 def expert_call(backward, where, near, last, rows, w_gate, w_up, w_down):
     wide = w_gate.shape[2]
     column = (META_B if backward else META_A) // META
     once = pl.Buffered(1)
-    in_specs = [pl.BlockSpec((ROWS, p.shape[1]), lambda i, w: (i, 0)) for p in near]
-    in_specs += [pl.BlockSpec(p.shape, lambda i, w: (0, 0), pipeline_mode=once) for p in last]
+    anywhere = pl.BlockSpec(memory_space=pl.ANY)
+    weights = [w_gate, w_up, w_down]
+    in_specs = [anywhere] * 6
     in_specs += [
         pl.BlockSpec((ROWS, META), lambda i, w: (0, column), pipeline_mode=once) for _ in rows
     ]
-    weights = [w_gate, w_up, w_down]
-    in_specs += [
-        pl.BlockSpec(p.shape, lambda i, w: (0, 0, 0), pipeline_mode=once) for p in weights
+    in_specs += [anywhere] * 3
+    width = 4 * HALF if backward else 8 * HALF
+    out_specs = [pl.BlockSpec((ROWS, HALF), lambda i, w: (i, 0))] * 4 if backward else []
+    out_specs += [
+        pl.BlockSpec((ROWS, width), lambda i, w: (0, 0), pipeline_mode=once) for _ in rows
     ]
-    out_specs = [pl.BlockSpec((ROWS, HALF), lambda i, w: (i, 0))] * 4
-    out_specs += [
-        pl.BlockSpec((ROWS, 4 * HALF), lambda i, w: (0, 0), pipeline_mode=once) for _ in rows
-    ]
-    out_shape = [jax.ShapeDtypeStruct((2 * ROWS, HALF), BF16)] * 4
-    out_shape += [jax.ShapeDtypeStruct((ROWS, 4 * HALF), BF16)] * 2
-    laid = pltpu.VMEM((ROWS, 8 * HALF), BF16)
+    out_shape = [jax.ShapeDtypeStruct((2 * ROWS, HALF), BF16)] * 4 if backward else []
+    out_shape += [jax.ShapeDtypeStruct((ROWS, width), BF16)] * 2
+    laid = [pltpu.VMEM((2, ROWS, 8 * HALF), BF16), pltpu.SemaphoreType.DMA((2, 8))]
     narrow = pltpu.VMEM((ROWS, wide), BF16)
+    scratch = [pltpu.VMEM(p.shape, BF16) for p in weights] + [pltpu.SemaphoreType.DMA((3,))]
+    scratch += laid + laid + [narrow] * 2 if backward else laid + [narrow]
     products = 5 if backward else 3
-    outs = pl.pallas_call(
+    return pl.pallas_call(
         backward_kernel if backward else forward_kernel,
         grid_spec=pltpu.PrefetchScalarGridSpec(
             num_scalar_prefetch=1,
             grid=(2,),
             in_specs=in_specs,
             out_specs=out_specs,
-            scratch_shapes=[laid, laid, narrow, narrow] if backward else [laid, narrow],
+            scratch_shapes=scratch,
         ),
         out_shape=out_shape,
-        compiler_params=params(44 if backward else 34),
+        compiler_params=params(46 if backward else 40),
         cost_estimate=cost(
             2 * products * 2 * ROWS * 8 * HALF * wide, 30 * 2**20, 2 * ROWS * wide
         ),
     )(where, *near, *last, *rows, *weights)
-    return outs[:4], outs[4:]
 
 
 def weight_columns(idents, weights):
@@ -366,7 +442,7 @@
     place = lax.axis_index("expert").astype(jnp.int32)
     core = here % 2
     group = jnp.where(core == 0, here // 2 % 4, here // 8)
-    where = jnp.stack([place, here, here + 1 - 2 * core, group])
+    where = jnp.stack([place, here, here + 1 - 2 * core, group, 3 - 2 * core])
     meta = jnp.concatenate(weight_columns(ids_a, prob_a) + weight_columns(ids_b, prob_b), axis=1)
     inputs = (x_a, x_b, cot_b)
     def stack(parts):
@@ -389,10 +465,6 @@
         height = values.shape[0] // 4
         return [values[d * height : (d + 1) * height] for d in range(4)]
 
-    def slot_rows(slots, dense):
-        own, sibling = gather_last(where, slots, dense)
-        return own, swap(sibling)
-
     quarters = spread(jnp.concatenate([v[:, HALF:] for v in inputs], axis=1), DEPTH)
     first = spread(jnp.concatenate([v[:, :HALF] for v in inputs] + [meta], axis=1), FIRST)
     quarters, first = together(quarters, first)
@@ -403,41 +475,46 @@
 
     dense_a = gather_section(stack(whole_a))
     own, sibling, slots_a, slots_b = gather_first(where, near)
-    whole_b = spread(stack([q[:, HALF:] for q in quarters]), FIRST)
     rows = (own, swap(sibling))
     near_a = spread(stack([r[:, NEAR_A : NEAR_A + HALF] for r in rows]), DEPTH)
-    whole_b, near_a = together(whole_b, near_a)
+    whole_b = spread(stack([q[:, HALF:] for q in quarters]), FIRST)
+    whole_b, near_a, dense_a = together(whole_b, near_a, dense_a)
 
     dense_b = gather_section(stack(whole_b))
-    near_b = spread(stack([r[:, NEAR_B : NEAR_B + 2 * HALF] for r in rows]), DEPTH)
-    last_a = slot_rows(slots_a, dense_a)
-    near_a, (own, sibling) = expert_call(
-        False, where, near_a, last_a, rows, w_gate, w_up, w_down
+    own_a, sibling_a = gather_last(where, slots_a, dense_a)
+    near_b = around(stack([r[:, NEAR_B : NEAR_B + 2 * HALF] for r in rows]), 1)
+    near_b, sibling_a = together(near_b, swap(sibling_a))
+    near_b += around(near_b[1], 1)[1:]
+    own_a, sibling_a = expert_call(
+        False, where, near_a, (own_a, sibling_a), rows, w_gate, w_up, w_down
     )
-    dense_a = scatter_last(where, slots_a, own, swap(sibling))
-    near_b, dense_a = together(near_b, dense_a)
-
-    group_a = scatter_section(dense_a)
-    returned_a = collect(near_a, DEPTH)
-    last_b = slot_rows(slots_b, dense_b)
-    near_b, (own, sibling) = expert_call(True, where, near_b, last_b, rows, w_gate, w_up, w_down)
-    dense_b = scatter_last(where, slots_b, own, swap(sibling))
-    dense_b, returned_a = together(dense_b, returned_a)
-
-    group_b = scatter_section(dense_b)
-    returned_b = collect(near_b, DEPTH)
-    parts_a = scatter_first(slots_a, returned_a[:ROWS], swap(returned_a[ROWS:]))
-    first_a = collect(cut(collect(parts_a, LAST)), FIRST)
-    last_a = collect(cut(collect(cut(group_a), FIRST)), DEPTH)
-    first_a, last_a, returned_b = together(first_a, last_a, returned_b)
-
-    parts_b = scatter_first(slots_b, returned_b[:ROWS], swap(returned_b[ROWS:]))
-    group_b, parts_b = collect(cut(group_b), FIRST), collect(parts_b, LAST)
-    last_b, first_b = collect(cut(group_b), DEPTH), collect(cut(parts_b), FIRST)
-    return (
-        jnp.concatenate([first_a, last_a], axis=1),
-        jnp.concatenate([first_b, last_b], axis=1),
+    near_b, own_a, sibling_a = together(near_b, own_a, sibling_a)
+    near_b += around(near_b[2], 1)[1:]
+    near_b, sibling_a, dense_b = together(near_b, swap(sibling_a), dense_b)
+
+    group_a = scatter_section(scatter_last(where, slots_a, own_a, sibling_a))
+    own, sibling = gather_last(where, slots_b, dense_b)
+    sibling = swap(sibling)
+    *near_b, own_b, sibling_b = expert_call(
+        True, where, near_b, (own, sibling), rows, w_gate, w_up, w_down
     )
+    own_b, sibling_b = together(own_b, swap(sibling_b))
+
+    group_b = scatter_section(scatter_last(where, slots_b, own_b, sibling_b))
+    near_b = send(near_b, DEPTH)
+    group_a = send(cut(group_a), FIRST)
+    near_b, group_a = together(near_b, group_a)
+
+    returned_b = total(near_b)
+    quarters_a = send(cut(total(group_a)), DEPTH)
+    sibling_b, quarters_a, group_b = together(swap(returned_b[ROWS:]), quarters_a, group_b)
+
+    parts_b = send(scatter_first(slots_b, returned_b[:ROWS], sibling_b), LAST)
+    parts_b, group_b = together(parts_b, send(cut(group_b), FIRST))
+    first_b, last_b = together(
+        send(cut(total(parts_b)), FIRST), send(cut(total(group_b)), DEPTH)
+    )
+    return total(quarters_a), jnp.concatenate([total(first_b), total(last_b)], axis=1)
 
 
 def solution(mesh):

time: 379 us -> 325 us (0.86); the launches traced: 372 us -> 323 us
  waiting for transfers between devices: 175 us -> 146 us
  starting transfers between devices: 89.1 us -> 60.1 us
  local copies, waits for them, and re-layouts: 27.8 us -> 39.6 us
    ppermute x21 -> x18, waiting for transfers between devices: 106 us -> 52.1 us  [spread(): lax.ppermute(values, axis, shifts[4 - d])]
    ppermute x30 -> x24, starting transfers between devices: 58.3 us -> 30.8 us  [the longest x21 28.8 us: send(): lax.ppermute(parts[d], axis, shifts[d])]
    ppermute x30 -> x24, waiting for transfers between devices: 56.3 us -> 83.7 us  [the longest x21 50 us: send(): lax.ppermute(parts[d], axis, shifts[d])]
    unnamed x81 -> x85, local copies, waits for them, and re-layouts: 22.7 us -> 33 us
    ppermute x7 -> x6, waiting for transfers between devices: 11.9 us -> 8.39 us  [swap(): return lax.ppermute(values, 'section', SWAP)]
    ppermute x21 -> x18, starting transfers between devices: 29.4 us -> 28.3 us  [spread(): lax.ppermute(values, axis, shifts[4 - d])]
  transfers between devices with their start and end apart: 62 -> 52, of which waited for: 29 -> 28; matrix products, arithmetic and copies ran while one was open for 3% -> 3% of each run, Pallas kernels for 15% -> 15%
where the time goes in v2:
time: 325 us; the launch traced here: 323 us
  waiting for transfers between devices  146 us (45%)
  starting transfers between devices  60.1 us (18%)
  Pallas kernels  53.7 us (17%)
  local copies, waits for them, and re-layouts  39.6 us (12%)
  between operations  14.4 us (4%)
  other arithmetic  9.76 us (3%)
    ppermute x18, waiting for transfers between devices, spread(): lax.ppermute(values, axis, shifts[4 - d])  52.1 us
    ppermute x21, waiting for transfers between devices, send(): lax.ppermute(parts[d], axis, shifts[d])  50 us
    pallas_call x2, Pallas kernels, expert_call(): pl.pallas_call(backward_kernel if backward else forward_kernel, grid_spec...  38.2 us
    ppermute x3, waiting for transfers between devices, around(): parts.append(lax.ppermute(parts[-1], ('section', 'expert'), DEPTH_RING))  33.7 us
    unnamed x85, local copies, waits for them, and re-layouts  33 us
    ppermute x21, starting transfers between devices, send(): lax.ppermute(parts[d], axis, shifts[d])  28.8 us
    ppermute x18, starting transfers between devices, spread(): lax.ppermute(values, axis, shifts[4 - d])  28.3 us
    ppermute x6, waiting for transfers between devices, swap(): return lax.ppermute(values, 'section', SWAP)  8.39 us
  transfers between devices with their start and end apart: 52, of which 28 were waited for; matrix products, arithmetic and copies ran while one was open for 3% of the time, Pallas kernels for 15%

profile of v2, /device:TPU:16, one launch (start us, length us, event | category | flops | bytes accessed | tf_op | source)
XLA Modules:
  0.0 323.2 jit_solution(8002125962079727247)
XLA Ops:
  16.1 3.6 %collective-permute-start.1 = (bf16[64,1536]{1,0:T(8,128)(2,1)S(1)}, bf16[64,1536]{1,0:T(8,128)(2,1)S(1)}, u32[]{:S(2)}, u32[]{:S(2)}) collective-permute-start(bf16[64,1536]{1,0:T(8,128)(2,1)S(1)} %pad_maximum_fusion.6), channel_id=1, source_target_pairs={{0,2},{1,3},{2,0},{3,1},{4,6},{5,7},{6,4},{7,5},{8,10},{9,11},{10,... | collective-permute-start | bytes 589832 | tf_op jit(solution)/shard_map/ppermute | solution.py:64
  20.7 4.1 %collective-permute-done.1 = bf16[64,1536]{1,0:T(8,128)(2,1)S(1)} collective-permute-done((bf16[64,1536]{1,0:T(8,128)(2,1)S(1)}, bf16[64,1536]{1,0:T(8,128)(2,1)S(1)}, u32[]{:S(2)}, u32[]{:S(2)}) %collective-permute-start.1) | collective-permute-done | bytes 196640 | tf_op jit(solution)/shard_map/ppermute | solution.py:64
  24.7 3.6 %collective-permute-done = bf16[64,1536]{1,0:T(8,128)(2,1)S(1)} collective-permute-done((bf16[64,1536]{1,0:T(8,128)(2,1)S(1)}, bf16[64,1536]{1,0:T(8,128)(2,1)S(1)}, u32[]{:S(2)}, u32[]{:S(2)}) %collective-permute-start) | collective-permute-done | bytes 196640 | tf_op jit(solution)/shard_map/ppermute | solution.py:64
  35.4 7.5 %collective-permute-done.8 = bf16[256,512]{1,0:T(8,128)(2,1)S(1)} collective-permute-done((bf16[256,512]{1,0:T(8,128)(2,1)S(1)}, bf16[256,512]{1,0:T(8,128)(2,1)S(1)}, u32[]{:S(2)}, u32[]{:S(2)}) %collective-permute-start.8) | collective-permute-done | bytes 262176 | tf_op jit(solution)/shard_map/ppermute | solution.py:64
  43.1 5.2 %collective-permute-done.7 = bf16[256,512]{1,0:T(8,128)(2,1)S(1)} collective-permute-done((bf16[256,512]{1,0:T(8,128)(2,1)S(1)}, bf16[256,512]{1,0:T(8,128)(2,1)S(1)}, u32[]{:S(2)}, u32[]{:S(2)}) %collective-permute-start.7) | collective-permute-done | bytes 262176 | tf_op jit(solution)/shard_map/ppermute | solution.py:64
  48.3 3.8 %collective-permute-done.6 = bf16[256,512]{1,0:T(8,128)(2,1)S(1)} collective-permute-done((bf16[256,512]{1,0:T(8,128)(2,1)S(1)}, bf16[256,512]{1,0:T(8,128)(2,1)S(1)}, u32[]{:S(2)}, u32[]{:S(2)}) %collective-permute-start.6) | collective-permute-done | bytes 262176 | tf_op jit(solution)/shard_map/ppermute | solution.py:64
  52.1 5.1 %collective-permute-done.11.refs_3_ = bf16[256,1664]{1,0:T(8,128)(2,1)S(1)} collective-permute-done((bf16[256,1664]{1,0:T(8,128)(2,1)S(1)}, bf16[256,1664]{1,0:T(8,128)(2,1)S(1)}, u32[]{:S(2)}, u32[]{:S(2)}) %collective-permute-start.11) | collective-permute-done | bytes 852000 | tf_op jit(solution)/shard_map/ppermute | solution.py:64
  62.7 2.5 shard_map.113
  75.8 3.4 %collective-permute-start.14 = (bf16[256,1024]{1,0:T(8,128)(2,1)S(1)}, bf16[256,1024]{1,0:T(8,128)(2,1)S(1)}, u32[]{:S(2)}, u32[]{:S(2)}) collective-permute-start(bf16[256,1024]{1,0:T(8,128)(2,1)S(1)} %pad_maximum_fusion.4), channel_id=1, source_target_pairs={{0,96},{4,28},{8,104},{12,4},{16,112},{20,12},{24,120},{28,20},{32... | collective-permute-start | bytes 1572872 | tf_op jit(solution)/shard_map/ppermute | solution.py:64
  79.2 11.4 %collective-permute-done.15 = bf16[256,1024]{1,0:T(8,128)(2,1)S(1)} collective-permute-done((bf16[256,1024]{1,0:T(8,128)(2,1)S(1)}, bf16[256,1024]{1,0:T(8,128)(2,1)S(1)}, u32[]{:S(2)}, u32[]{:S(2)}) %collective-permute-start.15) | collective-permute-done | bytes 524320 | tf_op jit(solution)/shard_map/ppermute | solution.py:64
  90.6 11.0 %collective-permute-done.14 = bf16[256,1024]{1,0:T(8,128)(2,1)S(1)} collective-permute-done((bf16[256,1024]{1,0:T(8,128)(2,1)S(1)}, bf16[256,1024]{1,0:T(8,128)(2,1)S(1)}, u32[]{:S(2)}, u32[]{:S(2)}) %collective-permute-start.14) | collective-permute-done | bytes 524320 | tf_op jit(solution)/shard_map/ppermute | solution.py:64
  105.8 3.1 pad_maximum_fusion
  113.7 14.4 %collective-permute-done.13.refs_1_ = bf16[640,1024]{1,0:T(8,128)(2,1)S(1)} collective-permute-done((bf16[640,1024]{1,0:T(8,128)(2,1)S(1)}, bf16[640,1024]{1,0:T(8,128)(2,1)S(1)}, u32[]{:S(2)}, u32[]{:S(2)}) %collective-permute-start.13) | collective-permute-done | bytes 1310752 | tf_op jit(solution)/shard_map/ppermute | solution.py:75
  128.4 15.4 %shard_map.115 = (bf16[320,4096]{1,0:T(8,128)(2,1)S(1)}, bf16[320,4096]{1,0:T(8,128)(2,1)S(1)}) custom-call(s32[5]{0:T(128)S(1)} %stack.23.where, bf16[640,512]{1,0:T(8,128)(2,1)S(1)} %pad_maximum_fusion.3.refs_0_, bf16[640,512]{1,0:T(8,128)(2,1)S(1)} %copy-done.21, bf16[640,512]{1,0:T(8,128)(2,1)S(1)} %copy-done.19, bf16[640,512]{1,0:T(8,128)(2,1)S(1)} %copy-done.17, ...), custom_call_target="tpu_custom_call" | custom-call | flops 125829120 | bytes 491520 | tf_op jit(solution)/shard_map/pallas_call | solution.py:414
  148.0 17.8 %collective-permute-done.22.refs_3_ = bf16[640,1024]{1,0:T(8,128)(2,1)S(1)} collective-permute-done((bf16[640,1024]{1,0:T(8,128)(2,1)S(1)}, bf16[640,1024]{1,0:T(8,128)(2,1)S(1)}, u32[]{:S(2)}, u32[]{:S(2)}) %collective-permute-start.22) | collective-permute-done | bytes 1310752 | tf_op jit(solution)/shard_map/ppermute | solution.py:75
  172.9 3.5 %shard_map.118 = bf16[4096,1024]{1,0:T(8,128)(2,1)S(1)} custom-call(s32[5]{0:T(128)S(1)} %stack.23.where, bf16[4,160,256]{2,1,0:T(8,128)(2,1)S(1)} %copy-done.11, bf16[320,4096]{1,0:T(8,128)(2,1)S(1)} %copy-done.5, bf16[320,4096]{1,0:T(8,128)(2,1)S(1)} %copy-done.7), custom_call_target="tpu_custom_call" | custom-call | flops 20971520 | bytes 458752 | tf_op jit(solution)/shard_map/pallas_call | solution.py:243
  176.5 3.3 %copy-done = bf16[4096,1024]{1,0:T(8,128)(2,1)} copy-done((bf16[4096,1024]{1,0:T(8,128)(2,1)}, bf16[4096,1024]{1,0:T(8,128)(2,1)S(1)}, u32[]{:S(2)}) %copy-start) | copy-done | bytes 8388632
  179.8 3.4 %copy-done.2 = bf16[4096,1024]{1,0:T(8,128)(2,1)S(1)} copy-done((bf16[4096,1024]{1,0:T(8,128)(2,1)S(1)}, bf16[4096,1024]{1,0:T(8,128)(2,1)}, u32[]{:S(2)}) %copy-start.2) | copy-done | bytes 8388632
  183.2 4.5 %shard_map.116 = (bf16[320,4096]{1,0:T(8,128)(2,1)S(1)}, bf16[320,4096]{1,0:T(8,128)(2,1)S(1)}) custom-call(s32[5]{0:T(128)S(1)} %stack.23.where, bf16[4,160,256]{2,1,0:T(8,128)(2,1)S(1)} %get-tuple-element.136.slots_ref, bf16[4096,1024]{1,0:T(8,128)(2,1)S(1)} %copy-done.2), custom_call_target="tpu_custom_call" | custom-call | flops 20971520 | bytes 458752 | tf_op jit(solution)/shard_map/pallas_call | solution.py:193
  189.2 4.9 %collective-permute-done.24.refs_5_ = bf16[320,4096]{1,0:T(8,128)(2,1)S(1)} collective-permute-done((bf16[320,4096]{1,0:T(8,128)(2,1)S(1)}, bf16[320,4096]{1,0:T(8,128)(2,1)S(1)}, u32[]{:S(2)}, u32[]{:S(2)}) %collective-permute-start.24) | collective-permute-done | bytes 2621472 | tf_op jit(solution)/shard_map/ppermute | solution.py:92
  195.6 22.8 %shard_map.117 = (bf16[640,512]{1,0:T(8,128)(2,1)S(1)}, bf16[640,512]{1,0:T(8,128)(2,1)S(1)}, bf16[640,512]{1,0:T(8,128)(2,1)S(1)}, bf16[640,512]{1,0:T(8,128)(2...) custom-call(s32[5]{0:T(128)S(1)} %stack.23.where, bf16[640,1024]{1,0:T(8,128)(2,1)} %copy-done.28, ...), custom_call_target="tpu_custom_call" | custom-call | flops 209715200 | bytes 491520 | tf_op jit(solution)/shard_map/pallas_call | solution.py:414
  221.2 2.8 collective-permute-done.35.sibling_ref
  224.0 2.5 shard_map.119
  235.3 2.7 collective-permute-start.29
  238.0 23.9 %collective-permute-done.25 = bf16[640,512]{1,0:T(8,128)(2,1)} collective-permute-done((bf16[640,512]{1,0:T(8,128)(2,1)S(1)}, bf16[640,512]{1,0:T(8,128)(2,1)}, u32[]{:S(2)}, u32[]{:S(2)}) %collective-permute-start.25) | collective-permute-done | bytes 655392 | tf_op jit(solution)/shard_map/ppermute | solution.py:81
  263.2 7.9 %collective-permute-done.28 = bf16[256,1024]{1,0:T(8,128)(2,1)S(1)} collective-permute-done((bf16[256,1024]{1,0:T(8,128)(2,1)S(1)}, bf16[256,1024]{1,0:T(8,128)(2,1)S(1)}, u32[]{:S(2)}, u32[]{:S(2)}) %collective-permute-start.28) | collective-permute-done | bytes 524320 | tf_op jit(solution)/shard_map/ppermute | solution.py:81
  276.0 4.2 %collective-permute-done.34 = bf16[64,1024]{1,0:T(8,128)(2,1)S(1)} collective-permute-done((bf16[64,1024]{1,0:T(8,128)(2,1)S(1)}, bf16[64,1024]{1,0:T(8,128)(2,1)S(1)}, u32[]{:S(2)}, u32[]{:S(2)}) %collective-permute-start.34) | collective-permute-done | bytes 131104 | tf_op jit(solution)/shard_map/ppermute | solution.py:81
  280.2 2.7 collective-permute-done.33
  291.4 2.9 collective-permute-start.40
  295.5 3.6 %collective-permute-start.39 = (bf16[256,512]{1,0:T(8,128)(2,1)S(1)}, bf16[256,512]{1,0:T(8,128)(2,1)S(1)}, u32[]{:S(2)}, u32[]{:S(2)}) collective-permute-start(bf16[256,512]{1,0:T(8,128)(2,1)S(1)} %get-tuple-element.190), channel_id=1, source_target_pairs={{0,32},{4,12},{8,40},{12,20},{16,48},{20,28},{24,56},{28,4},{32,64... | collective-permute-start | bytes 786440 | tf_op jit(solution)/shard_map/ppermute | solution.py:81
  300.3 2.6 collective-permute-done.39
  303.2 4.5 %collective-permute-start.43 = (bf16[64,512]{1,0:T(8,128)(2,1)S(1)}, bf16[64,512]{1,0:T(8,128)(2,1)S(1)}, u32[]{:S(2)}, u32[]{:S(2)}) collective-permute-start(bf16[64,512]{1,0:T(8,128)(2,1)S(1)} %get-tuple-element.203), channel_id=1, source_target_pairs={{0,64},{4,20},{8,72},{12,28},{16,80},{20,4},{24,88},{28,12},{32,96... | collective-permute-start | bytes 196616 | tf_op jit(solution)/shard_map/ppermute | solution.py:81
  (219 shorter events, 94.3 us)
Async XLA Ops:
  7.2 98.6 %all-gather.3.cloned.1.call-start = ((), (), s32[]{:S(2)}) async-start(), calls=%async_computation.2 | async-start | bytes 5242880 | tf_op jit(solution)/shard_map/all_gather | solution.py:455
  9.1 10.6 %collective-permute-start.2 = (bf16[64,1536]{1,0:T(8,128)(2,1)S(1)}, bf16[64,1536]{1,0:T(8,128)(2,1)S(1)}, u32[]{:S(2)}, u32[]{:S(2)}) collective-permute-start(bf16[64,1536]{1,0:T(8,128)(2,1)S(1)} %pad_maximum_fusion.6), channel_id=1, source_target_pairs={{0,1},{1,2},{2,3},{3,0},{4,5},{5,6},{6,7},{7,4},{8,9},{9,10},{10,1... | collective-permute-start | bytes 589832 | tf_op jit(solution)/shard_map/ppermute | solution.py:64
  13.0 15.3 %collective-permute-start.5 = (bf16[64,1664]{1,0:T(8,128)(2,1)S(1)}, bf16[64,1664]{1,0:T(8,128)(2,1)S(1)}, u32[]{:S(2)}, u32[]{:S(2)}) collective-permute-start(bf16[64,1664]{1,0:T(8,128)(2,1)S(1)} %concatenate.31), channel_id=1, source_target_pairs={{0,32},{4,12},{8,40},{12,20},{16,48},{20,28},{24,56},{28,4},{32,64... | collective-permute-start | bytes 638984 | tf_op jit(solution)/shard_map/ppermute | solution.py:64
  14.4 14.0 %collective-permute-start.4 = (bf16[64,1664]{1,0:T(8,128)(2,1)S(1)}, bf16[64,1664]{1,0:T(8,128)(2,1)S(1)}, u32[]{:S(2)}, u32[]{:S(2)}) collective-permute-start(bf16[64,1664]{1,0:T(8,128)(2,1)S(1)} %concatenate.31), channel_id=1, source_target_pairs={{0,64},{4,20},{8,72},{12,28},{16,80},{20,4},{24,88},{28,12},{32,96... | collective-permute-start | bytes 638984 | tf_op jit(solution)/shard_map/ppermute | solution.py:64
  15.0 13.4 %collective-permute-start.3 = (bf16[64,1664]{1,0:T(8,128)(2,1)S(1)}, bf16[64,1664]{1,0:T(8,128)(2,1)S(1)}, u32[]{:S(2)}, u32[]{:S(2)}) collective-permute-start(bf16[64,1664]{1,0:T(8,128)(2,1)S(1)} %concatenate.31), channel_id=1, source_target_pairs={{0,96},{4,28},{8,104},{12,4},{16,112},{20,12},{24,120},{28,20},{32... | collective-permute-start | bytes 638984 | tf_op jit(solution)/shard_map/ppermute | solution.py:64
  28.5 28.7 %collective-permute-start.11 = (bf16[256,1664]{1,0:T(8,128)(2,1)S(1)}, bf16[256,1664]{1,0:T(8,128)(2,1)S(1)}, u32[]{:S(2)}, u32[]{:S(2)}) collective-permute-start(bf16[256,1664]{1,0:T(8,128)(2,1)S(1)} %constant_dynamic-update-slice_fusion.refs_0_), channel_id=1, source_target_pairs={{0,8},{4,36},{8,16},{12,44},{16,24},{20,52},{24,0},{28,60},{32,40}... | collective-permute-start | bytes 2555912 | tf_op jit(solution)/shard_map/ppermute | solution.py:64
  30.6 26.6 %collective-permute-start.10 = (bf16[256,1664]{1,0:T(8,128)(2,1)S(1)}, bf16[256,1664]{1,0:T(8,128)(2,1)S(1)}, u32[]{:S(2)}, u32[]{:S(2)}) collective-permute-start(bf16[256,1664]{1,0:T(8,128)(2,1)S(1)} %constant_dynamic-update-slice_fusion.refs_0_), channel_id=1, source_target_pairs={{0,16},{4,68},{8,24},{12,76},{16,0},{20,84},{24,8},{28,92},{32,48}... | collective-permute-start | bytes 2555912 | tf_op jit(solution)/shard_map/ppermute | solution.py:64
  31.7 26.5 %collective-permute-start.9 = (bf16[256,1664]{1,0:T(8,128)(2,1)S(1)}, bf16[256,1664]{1,0:T(8,128)(2,1)S(1)}, u32[]{:S(2)}, u32[]{:S(2)}) collective-permute-start(bf16[256,1664]{1,0:T(8,128)(2,1)S(1)} %constant_dynamic-update-slice_fusion.refs_0_), channel_id=1, source_target_pairs={{0,24},{4,100},{8,0},{12,108},{16,8},{20,116},{24,16},{28,124},{32... | collective-permute-start | bytes 2555912 | tf_op jit(solution)/shard_map/ppermute | solution.py:64
  34.8 13.5 %collective-permute-start.7 = (bf16[256,512]{1,0:T(8,128)(2,1)S(1)}, bf16[256,512]{1,0:T(8,128)(2,1)S(1)}, u32[]{:S(2)}, u32[]{:S(2)}) collective-permute-start(bf16[256,512]{1,0:T(8,128)(2,1)S(1)} %pad_maximum_fusion.5), channel_id=1, source_target_pairs={{0,64},{4,20},{8,72},{12,28},{16,80},{20,4},{24,88},{28,12},{32,96... | collective-permute-start | bytes 786440 | tf_op jit(solution)/shard_map/ppermute | solution.py:64
  60.2 108.3 %all-gather.5.cloned.1.call-start = ((), (), s32[]{:S(2)}) async-start(), calls=%async_computation.3 | async-start | bytes 10485760 | tf_op jit(solution)/shard_map/all_gather | solution.py:455
  68.2 33.5 %collective-permute-start.19 = (bf16[640,512]{1,0:T(8,128)(2,1)S(1)}, bf16[640,512]{1,0:T(8,128)(2,1)S(1)}, u32[]{:S(2)}, u32[]{:S(2)}) collective-permute-start(bf16[640,512]{1,0:T(8,128)(2,1)S(1)} %pad_maximum_fusion.3.refs_0_), channel_id=1, source_target_pairs={{0,1},{1,2},{2,3},{3,0},{4,5},{5,6},{6,7},{7,4},{8,9},{9,10},{10,1... | collective-permute-start | bytes 1966088 | tf_op jit(solution)/shard_map/ppermute | solution.py:64
  70.6 31.9 %collective-permute-start.18 = (bf16[640,512]{1,0:T(8,128)(2,1)S(1)}, bf16[640,512]{1,0:T(8,128)(2,1)S(1)}, u32[]{:S(2)}, u32[]{:S(2)}) collective-permute-start(bf16[640,512]{1,0:T(8,128)(2,1)S(1)} %pad_maximum_fusion.3.refs_0_), channel_id=1, source_target_pairs={{0,2},{1,3},{2,0},{3,1},{4,6},{5,7},{6,4},{7,5},{8,10},{9,11},{10,... | collective-permute-start | bytes 1966088 | tf_op jit(solution)/shard_map/ppermute | solution.py:64
  73.1 30.4 %collective-permute-start.17 = (bf16[640,512]{1,0:T(8,128)(2,1)S(1)}, bf16[640,512]{1,0:T(8,128)(2,1)S(1)}, u32[]{:S(2)}, u32[]{:S(2)}) collective-permute-start(bf16[640,512]{1,0:T(8,128)(2,1)S(1)} %pad_maximum_fusion.3.refs_0_), channel_id=1, source_target_pairs={{0,3},{1,0},{2,1},{3,2},{4,7},{5,4},{6,5},{7,6},{8,11},{9,8},{10,9... | collective-permute-start | bytes 1966088 | tf_op jit(solution)/shard_map/ppermute | solution.py:64
  74.3 16.3 %collective-permute-start.15 = (bf16[256,1024]{1,0:T(8,128)(2,1)S(1)}, bf16[256,1024]{1,0:T(8,128)(2,1)S(1)}, u32[]{:S(2)}, u32[]{:S(2)}) collective-permute-start(bf16[256,1024]{1,0:T(8,128)(2,1)S(1)} %pad_maximum_fusion.4), channel_id=1, source_target_pairs={{0,64},{4,20},{8,72},{12,28},{16,80},{20,4},{24,88},{28,12},{32,96... | collective-permute-start | bytes 1572872 | tf_op jit(solution)/shard_map/ppermute | solution.py:64
  75.8 25.9 %collective-permute-start.14 = (bf16[256,1024]{1,0:T(8,128)(2,1)S(1)}, bf16[256,1024]{1,0:T(8,128)(2,1)S(1)}, u32[]{:S(2)}, u32[]{:S(2)}) collective-permute-start(bf16[256,1024]{1,0:T(8,128)(2,1)S(1)} %pad_maximum_fusion.4), channel_id=1, source_target_pairs={{0,96},{4,28},{8,104},{12,4},{16,112},{20,12},{24,120},{28,20},{32... | collective-permute-start | bytes 1572872 | tf_op jit(solution)/shard_map/ppermute | solution.py:64
  108.9 124.1 %reduce-scatter.3.cloned.1.call-start = ((), (), s32[]{:S(2)}) async-start(), calls=%async_computation.4 | async-start | bytes 10485760 | tf_op jit(solution)/shard_map/reduce_scatter | solution.py:460
  109.2 18.9 %collective-permute-start.13 = (bf16[640,1024]{1,0:T(8,128)(2,1)S(1)}, bf16[640,1024]{1,0:T(8,128)(2,1)S(1)}, u32[]{:S(2)}, u32[]{:S(2)}) collective-permute-start(bf16[640,1024]{1,0:T(8,128)(2,1)S(1)} %pad_maximum_fusion.1.refs_0_), channel_id=1, source_target_pairs={{0,1},{1,2},{2,3},{3,0},{4,7},{5,4},{6,5},{7,6},{8,9},{9,10},{10,1... | collective-permute-start | bytes 3932168 | tf_op jit(solution)/shard_map/ppermute | solution.py:75
  113.6 14.5 %collective-permute-start.20 = (bf16[320,2048]{1,0:T(8,128)(2,1)S(1)}, bf16[320,2048]{1,0:T(8,128)(2,1)S(1)}, u32[]{:S(2)}, u32[]{:S(2)}) collective-permute-start(bf16[320,2048]{1,0:T(8,128)(2,1)S(1)} %get-tuple-element.113), channel_id=1, source_target_pairs={{0,4},{4,0},{8,12},{12,8},{16,20},{20,16},{24,28},{28,24},{32,36},... | collective-permute-start | bytes 3932168 | tf_op jit(solution)/shard_map/ppermute | solution.py:92
  128.1 18.8 %collective-permute-start.21 = (bf16[640,1024]{1,0:T(8,128)(2,1)S(1)}, bf16[640,1024]{1,0:T(8,128)(2,1)S(1)}, u32[]{:S(2)}, u32[]{:S(2)}) collective-permute-start(bf16[640,1024]{1,0:T(8,128)(2,1)S(1)} %collective-permute-done.13.refs_1_), channel_id=1, source_target_pairs={{0,1},{1,2},{2,3},{3,0},{4,7},{5,4},{6,5},{7,6},{8,9},{9,10},{10,1... | collective-permute-start | bytes 3932168 | tf_op jit(solution)/shard_map/ppermute | solution.py:75
  146.9 20.0 %collective-permute-start.23 = (bf16[320,4096]{1,0:T(8,128)(2,1)S(1)}, bf16[320,4096]{1,0:T(8,128)(2,1)S(1)}, u32[]{:S(2)}, u32[]{:S(2)}) collective-permute-start(bf16[320,4096]{1,0:T(8,128)(2,1)S(1)} %get-tuple-element.127), channel_id=1, source_target_pairs={{0,4},{4,0},{8,12},{12,8},{16,20},{20,16},{24,28},{28,24},{32,36},... | collective-permute-start | bytes 7864328 | tf_op jit(solution)/shard_map/ppermute | solution.py:92
  146.9 18.8 %collective-permute-start.22 = (bf16[640,1024]{1,0:T(8,128)(2,1)S(1)}, bf16[640,1024]{1,0:T(8,128)(2,1)S(1)}, u32[]{:S(2)}, u32[]{:S(2)}) collective-permute-start(bf16[640,1024]{1,0:T(8,128)(2,1)S(1)} %collective-permute-done.21.refs_2_), channel_id=1, source_target_pairs={{0,1},{1,2},{2,3},{3,0},{4,7},{5,4},{6,5},{7,6},{8,9},{9,10},{10,1... | collective-permute-start | bytes 3932168 | tf_op jit(solution)/shard_map/ppermute | solution.py:75
  179.8 96.2 %reduce-scatter.5.cloned.1.call-start = ((), (), s32[]{:S(2)}) async-start(), calls=%async_computation.5 | async-start | bytes 5242880 | tf_op jit(solution)/shard_map/reduce_scatter | solution.py:460
  229.6 32.3 %collective-permute-start.25 = (bf16[640,512]{1,0:T(8,128)(2,1)S(1)}, bf16[640,512]{1,0:T(8,128)(2,1)}, u32[]{:S(2)}, u32[]{:S(2)}) collective-permute-start(bf16[640,512]{1,0:T(8,128)(2,1)S(1)} %copy-done.27), channel_id=1, source_target_pairs={{0,1},{1,2},{2,3},{3,0},{4,5},{5,6},{6,7},{7,4},{8,9},{9,10},{10,1... | collective-permute-start | bytes 1966088 | tf_op jit(solution)/shard_map/ppermute | solution.py:81
  229.8 33.3 %collective-permute-start.26 = (bf16[640,512]{1,0:T(8,128)(2,1)S(1)}, bf16[640,512]{1,0:T(8,128)(2,1)}, u32[]{:S(2)}, u32[]{:S(2)}) collective-permute-start(bf16[640,512]{1,0:T(8,128)(2,1)S(1)} %copy-done.25), channel_id=1, source_target_pairs={{0,2},{1,3},{2,0},{3,1},{4,6},{5,7},{6,4},{7,5},{8,10},{9,11},{10,... | collective-permute-start | bytes 1966088 | tf_op jit(solution)/shard_map/ppermute | solution.py:81
  231.4 31.7 %collective-permute-start.27 = (bf16[640,512]{1,0:T(8,128)(2,1)S(1)}, bf16[640,512]{1,0:T(8,128)(2,1)}, u32[]{:S(2)}, u32[]{:S(2)}) collective-permute-start(bf16[640,512]{1,0:T(8,128)(2,1)S(1)} %copy-done.23), channel_id=1, source_target_pairs={{0,3},{1,0},{2,1},{3,2},{4,7},{5,4},{6,5},{7,6},{8,11},{9,8},{10,9... | collective-permute-start | bytes 1966088 | tf_op jit(solution)/shard_map/ppermute | solution.py:81
  234.7 28.5 %collective-permute-start.30 = (bf16[256,1024]{1,0:T(8,128)(2,1)S(1)}, bf16[256,1024]{1,0:T(8,128)(2,1)S(1)}, u32[]{:S(2)}, u32[]{:S(2)}) collective-permute-start(bf16[256,1024]{1,0:T(8,128)(2,1)S(1)} %get-tuple-element.184), channel_id=1, source_target_pairs={{0,96},{4,28},{8,104},{12,4},{16,112},{20,12},{24,120},{28,20},{32... | collective-permute-start | bytes 1572872 | tf_op jit(solution)/shard_map/ppermute | solution.py:81
  235.3 27.9 %collective-permute-start.29 = (bf16[256,1024]{1,0:T(8,128)(2,1)S(1)}, bf16[256,1024]{1,0:T(8,128)(2,1)S(1)}, u32[]{:S(2)}, u32[]{:S(2)}) collective-permute-start(bf16[256,1024]{1,0:T(8,128)(2,1)S(1)} %get-tuple-element.185), channel_id=1, source_target_pairs={{0,64},{4,20},{8,72},{12,28},{16,80},{20,4},{24,88},{28,12},{32,96... | collective-permute-start | bytes 1572872 | tf_op jit(solution)/shard_map/ppermute | solution.py:81
  273.0 11.6 %collective-permute-start.31 = (bf16[320,512]{1,0:T(8,128)(2,1)S(1)}, bf16[320,512]{1,0:T(8,128)(2,1)S(1)}, u32[]{:S(2)}, u32[]{:S(2)}) collective-permute-start(bf16[320,512]{1,0:T(8,128)(2,1)S(1)} %get-tuple-element.193), channel_id=1, source_target_pairs={{0,4},{4,0},{8,12},{12,8},{16,20},{20,16},{24,28},{28,24},{32,36},... | collective-permute-start | bytes 983048 | tf_op jit(solution)/shard_map/ppermute | solution.py:92
  285.0 10.5 %collective-permute-start.36 = (bf16[256,512]{1,0:T(8,128)(2,1)S(1)}, bf16[256,512]{1,0:T(8,128)(2,1)S(1)}, u32[]{:S(2)}, u32[]{:S(2)}) collective-permute-start(bf16[256,512]{1,0:T(8,128)(2,1)S(1)} %get-tuple-element.164), channel_id=1, source_target_pairs={{0,8},{4,36},{8,16},{12,44},{16,24},{20,52},{24,0},{28,60},{32,40}... | collective-permute-start | bytes 786440 | tf_op jit(solution)/shard_map/ppermute | solution.py:81
  285.9 13.2 %collective-permute-start.37 = (bf16[256,512]{1,0:T(8,128)(2,1)S(1)}, bf16[256,512]{1,0:T(8,128)(2,1)S(1)}, u32[]{:S(2)}, u32[]{:S(2)}) collective-permute-start(bf16[256,512]{1,0:T(8,128)(2,1)S(1)} %get-tuple-element.165), channel_id=1, source_target_pairs={{0,16},{4,68},{8,24},{12,76},{16,0},{20,84},{24,8},{28,92},{32,48}... | collective-permute-start | bytes 786440 | tf_op jit(solution)/shard_map/ppermute | solution.py:81
  287.9 12.4 %collective-permute-start.38 = (bf16[256,512]{1,0:T(8,128)(2,1)S(1)}, bf16[256,512]{1,0:T(8,128)(2,1)S(1)}, u32[]{:S(2)}, u32[]{:S(2)}) collective-permute-start(bf16[256,512]{1,0:T(8,128)(2,1)S(1)} %get-tuple-element.166), channel_id=1, source_target_pairs={{0,24},{4,100},{8,0},{12,108},{16,8},{20,116},{24,16},{28,124},{32... | collective-permute-start | bytes 786440 | tf_op jit(solution)/shard_map/ppermute | solution.py:81
  290.9 9.5 %collective-permute-start.41 = (bf16[256,512]{1,0:T(8,128)(2,1)S(1)}, bf16[256,512]{1,0:T(8,128)(2,1)S(1)}, u32[]{:S(2)}, u32[]{:S(2)}) collective-permute-start(bf16[256,512]{1,0:T(8,128)(2,1)S(1)} %get-tuple-element.188), channel_id=1, source_target_pairs={{0,96},{4,28},{8,104},{12,4},{16,112},{20,12},{24,120},{28,20},{32... | collective-permute-start | bytes 786440 | tf_op jit(solution)/shard_map/ppermute | solution.py:81
  (64 other events, 447.8 us)
Sparse Core Ops, SparseCore 0:
  60.3 45.4 all-gather.2
  109.0 50.2 all-gather.4
  179.9 45.5 reduce-scatter.2
  228.7 39.5 reduce-scatter.4

commit v3 on v2

--- a/solution.py
+++ b/solution.py
@@ -501,20 +501,19 @@
     own_b, sibling_b = together(own_b, swap(sibling_b))
 
     group_b = scatter_section(scatter_last(where, slots_b, own_b, sibling_b))
-    near_b = send(near_b, DEPTH)
-    group_a = send(cut(group_a), FIRST)
-    near_b, group_a = together(near_b, group_a)
+    near_b = together(*send(near_b, DEPTH))
 
     returned_b = total(near_b)
-    quarters_a = send(cut(total(group_a)), DEPTH)
-    sibling_b, quarters_a, group_b = together(swap(returned_b[ROWS:]), quarters_a, group_b)
+    sibling_b, group_a, group_b = together(swap(returned_b[ROWS:]), group_a, group_b)
 
     parts_b = send(scatter_first(slots_b, returned_b[:ROWS], sibling_b), LAST)
-    parts_b, group_b = together(parts_b, send(cut(group_b), FIRST))
-    first_b, last_b = together(
-        send(cut(total(parts_b)), FIRST), send(cut(total(group_b)), DEPTH)
-    )
-    return total(quarters_a), jnp.concatenate([total(first_b), total(last_b)], axis=1)
+    pairs = zip(cut(group_a), cut(group_b))
+    whole = send([jnp.concatenate(pair, axis=1) for pair in pairs], FIRST)
+    parts_b, whole = together(parts_b, whole)
+
+    first_b, last = together(send(cut(total(parts_b)), FIRST), send(cut(total(whole)), DEPTH))
+    last = total(last)
+    return last[:, : 2 * HALF], jnp.concatenate([total(first_b), last[:, 2 * HALF :]], axis=1)
 
 
 def solution(mesh):

time: 325 us -> 350 us (1.077)
  waiting for transfers between devices: 146 us -> 184 us
  starting transfers between devices: 60.1 us -> 50.1 us
    reduce_scatter x2, waiting for transfers between devices: 0.01 us -> 31.1 us  [scatter_section(): lax.psum_scatter(dense, 'section', scatter_dimension=0, tiled=True, axis_...]
    ppermute x21 -> x15, starting transfers between devices: 28.8 us -> 20.5 us  [send(): lax.ppermute(parts[d], axis, shifts[d])]
    ppermute x21 -> x15, waiting for transfers between devices: 50 us -> 52.9 us  [send(): lax.ppermute(parts[d], axis, shifts[d])]
    unnamed x85 -> x89, local copies, waits for them, and re-layouts: 33 us -> 33.1 us
  transfers between devices with their start and end apart: 52 -> 46, of which waited for: 28 -> 27; matrix products, arithmetic and copies ran while one was open for 3% -> 1% of each run, Pallas kernels for 15% -> 7%
where the time goes in v3:
time: 350 us; the launch traced here: 347 us
  waiting for transfers between devices  184 us (53%)
  Pallas kernels  53.3 us (15%)
  starting transfers between devices  50.1 us (14%)
  local copies, waits for them, and re-layouts  38.1 us (11%)
  between operations  14.4 us (4%)
  other arithmetic  7.67 us (2%)
    ppermute x18, waiting for transfers between devices, spread(): lax.ppermute(values, axis, shifts[4 - d])  53.6 us
    ppermute x15, waiting for transfers between devices, send(): lax.ppermute(parts[d], axis, shifts[d])  52.9 us
    pallas_call x2, Pallas kernels, expert_call(): pl.pallas_call(backward_kernel if backward else forward_kernel, grid_spec...  37.8 us
    ppermute x3, waiting for transfers between devices, around(): parts.append(lax.ppermute(parts[-1], ('section', 'expert'), DEPTH_RING))  33.7 us
    unnamed x89, local copies, waits for them, and re-layouts  33.1 us
    reduce_scatter x2, waiting for transfers between devices, scatter_section(): lax.psum_scatter(dense, 'section', scatter_dimension=0, tiled=True, axis_...  31.1 us
    ppermute x18, starting transfers between devices, spread(): lax.ppermute(values, axis, shifts[4 - d])  26.8 us
    ppermute x15, starting transfers between devices, send(): lax.ppermute(parts[d], axis, shifts[d])  20.5 us
  transfers between devices with their start and end apart: 46, of which 27 were waited for; matrix products, arithmetic and copies ran while one was open for 1% of the time, Pallas kernels for 7%

profile of v3, /device:TPU:16, one launch (start us, length us, event | category | flops | bytes accessed | tf_op | source)
XLA Modules:
  0.0 347.3 jit_solution(187777106024376686)
XLA Ops:
  16.1 3.6 %collective-permute-start.1 = (bf16[64,1536]{1,0:T(8,128)(2,1)S(1)}, bf16[64,1536]{1,0:T(8,128)(2,1)S(1)}, u32[]{:S(2)}, u32[]{:S(2)}) collective-permute-start(bf16[64,1536]{1,0:T(8,128)(2,1)S(1)} %pad_maximum_fusion.10), channel_id=1, source_target_pairs={{0,2},{1,3},{2,0},{3,1},{4,6},{5,7},{6,4},{7,5},{8,10},{9,11},{10,... | collective-permute-start | bytes 589832 | tf_op jit(solution)/shard_map/ppermute | solution.py:64
  20.7 4.1 %collective-permute-done.1 = bf16[64,1536]{1,0:T(8,128)(2,1)S(1)} collective-permute-done((bf16[64,1536]{1,0:T(8,128)(2,1)S(1)}, bf16[64,1536]{1,0:T(8,128)(2,1)S(1)}, u32[]{:S(2)}, u32[]{:S(2)}) %collective-permute-start.1) | collective-permute-done | bytes 196640 | tf_op jit(solution)/shard_map/ppermute | solution.py:64
  24.7 3.6 %collective-permute-done = bf16[64,1536]{1,0:T(8,128)(2,1)S(1)} collective-permute-done((bf16[64,1536]{1,0:T(8,128)(2,1)S(1)}, bf16[64,1536]{1,0:T(8,128)(2,1)S(1)}, u32[]{:S(2)}, u32[]{:S(2)}) %collective-permute-start) | collective-permute-done | bytes 196640 | tf_op jit(solution)/shard_map/ppermute | solution.py:64
  35.4 7.5 %collective-permute-done.8 = bf16[256,512]{1,0:T(8,128)(2,1)S(1)} collective-permute-done((bf16[256,512]{1,0:T(8,128)(2,1)S(1)}, bf16[256,512]{1,0:T(8,128)(2,1)S(1)}, u32[]{:S(2)}, u32[]{:S(2)}) %collective-permute-start.8) | collective-permute-done | bytes 262176 | tf_op jit(solution)/shard_map/ppermute | solution.py:64
  43.1 5.2 %collective-permute-done.7 = bf16[256,512]{1,0:T(8,128)(2,1)S(1)} collective-permute-done((bf16[256,512]{1,0:T(8,128)(2,1)S(1)}, bf16[256,512]{1,0:T(8,128)(2,1)S(1)}, u32[]{:S(2)}, u32[]{:S(2)}) %collective-permute-start.7) | collective-permute-done | bytes 262176 | tf_op jit(solution)/shard_map/ppermute | solution.py:64
  48.3 3.8 %collective-permute-done.6 = bf16[256,512]{1,0:T(8,128)(2,1)S(1)} collective-permute-done((bf16[256,512]{1,0:T(8,128)(2,1)S(1)}, bf16[256,512]{1,0:T(8,128)(2,1)S(1)}, u32[]{:S(2)}, u32[]{:S(2)}) %collective-permute-start.6) | collective-permute-done | bytes 262176 | tf_op jit(solution)/shard_map/ppermute | solution.py:64
  52.1 5.1 %collective-permute-done.11.refs_3_ = bf16[256,1664]{1,0:T(8,128)(2,1)S(1)} collective-permute-done((bf16[256,1664]{1,0:T(8,128)(2,1)S(1)}, bf16[256,1664]{1,0:T(8,128)(2,1)S(1)}, u32[]{:S(2)}, u32[]{:S(2)}) %collective-permute-start.11) | collective-permute-done | bytes 852000 | tf_op jit(solution)/shard_map/ppermute | solution.py:64
  62.6 2.5 shard_map.113
  68.1 2.4 collective-permute-start.19
  70.6 2.4 collective-permute-start.18
  77.3 13.3 %collective-permute-done.15 = bf16[256,1024]{1,0:T(8,128)(2,1)S(1)} collective-permute-done((bf16[256,1024]{1,0:T(8,128)(2,1)S(1)}, bf16[256,1024]{1,0:T(8,128)(2,1)S(1)}, u32[]{:S(2)}, u32[]{:S(2)}) %collective-permute-start.15) | collective-permute-done | bytes 524320 | tf_op jit(solution)/shard_map/ppermute | solution.py:64
  90.6 11.0 %collective-permute-done.14 = bf16[256,1024]{1,0:T(8,128)(2,1)S(1)} collective-permute-done((bf16[256,1024]{1,0:T(8,128)(2,1)S(1)}, bf16[256,1024]{1,0:T(8,128)(2,1)S(1)}, u32[]{:S(2)}, u32[]{:S(2)}) %collective-permute-start.14) | collective-permute-done | bytes 524320 | tf_op jit(solution)/shard_map/ppermute | solution.py:64
  105.7 3.0 pad_maximum_fusion
  113.6 14.4 %collective-permute-done.13.refs_1_ = bf16[640,1024]{1,0:T(8,128)(2,1)S(1)} collective-permute-done((bf16[640,1024]{1,0:T(8,128)(2,1)S(1)}, bf16[640,1024]{1,0:T(8,128)(2,1)S(1)}, u32[]{:S(2)}, u32[]{:S(2)}) %collective-permute-start.13) | collective-permute-done | bytes 1310752 | tf_op jit(solution)/shard_map/ppermute | solution.py:75
  128.3 15.4 %shard_map.115 = (bf16[320,4096]{1,0:T(8,128)(2,1)S(1)}, bf16[320,4096]{1,0:T(8,128)(2,1)S(1)}) custom-call(s32[5]{0:T(128)S(1)} %stack.23.where, bf16[640,512]{1,0:T(8,128)(2,1)S(1)} %pad_maximum_fusion.7.refs_0_, bf16[640,512]{1,0:T(8,128)(2,1)S(1)} %copy-done.21, bf16[640,512]{1,0:T(8,128)(2,1)S(1)} %copy-done.19, bf16[640,512]{1,0:T(8,128)(2,1)S(1)} %copy-done.17, ...), custom_call_target="tpu_custom_call" | custom-call | flops 125829120 | bytes 491520 | tf_op jit(solution)/shard_map/pallas_call | solution.py:414
  147.9 17.7 %collective-permute-done.22.refs_3_ = bf16[640,1024]{1,0:T(8,128)(2,1)S(1)} collective-permute-done((bf16[640,1024]{1,0:T(8,128)(2,1)S(1)}, bf16[640,1024]{1,0:T(8,128)(2,1)S(1)}, u32[]{:S(2)}, u32[]{:S(2)}) %collective-permute-start.22) | collective-permute-done | bytes 1310752 | tf_op jit(solution)/shard_map/ppermute | solution.py:75
  168.3 3.4 copy-done.2
  171.7 4.5 %shard_map.116 = (bf16[320,4096]{1,0:T(8,128)(2,1)S(1)}, bf16[320,4096]{1,0:T(8,128)(2,1)S(1)}) custom-call(s32[5]{0:T(128)S(1)} %stack.23.where, bf16[4,160,256]{2,1,0:T(8,128)(2,1)S(1)} %get-tuple-element.98.slots_ref, bf16[4096,1024]{1,0:T(8,128)(2,1)S(1)} %copy-done.2), custom_call_target="tpu_custom_call" | custom-call | flops 20971520 | bytes 458752 | tf_op jit(solution)/shard_map/pallas_call | solution.py:193
  177.6 4.9 %collective-permute-done.24.refs_5_ = bf16[320,4096]{1,0:T(8,128)(2,1)S(1)} collective-permute-done((bf16[320,4096]{1,0:T(8,128)(2,1)S(1)}, bf16[320,4096]{1,0:T(8,128)(2,1)S(1)}, u32[]{:S(2)}, u32[]{:S(2)}) %collective-permute-start.24) | collective-permute-done | bytes 2621472 | tf_op jit(solution)/shard_map/ppermute | solution.py:92
  184.1 22.4 %shard_map.117 = (bf16[640,512]{1,0:T(8,128)(2,1)S(1)}, bf16[640,512]{1,0:T(8,128)(2,1)S(1)}, bf16[640,512]{1,0:T(8,128)(2,1)S(1)}, bf16[640,512]{1,0:T(8,128)(2...) custom-call(s32[5]{0:T(128)S(1)} %stack.23.where, bf16[640,1024]{1,0:T(8,128)(2,1)} %copy-done.28, ...), custom_call_target="tpu_custom_call" | custom-call | flops 209715200 | bytes 491520 | tf_op jit(solution)/shard_map/pallas_call | solution.py:414
  209.2 2.9 collective-permute-done.29.sibling_ref
  212.1 2.5 shard_map.119
  221.1 3.5 %shard_map.118 = bf16[4096,1024]{1,0:T(8,128)(2,1)S(1)} custom-call(s32[5]{0:T(128)S(1)} %stack.23.where, bf16[4,160,256]{2,1,0:T(8,128)(2,1)S(1)} %copy-done.11, bf16[320,4096]{1,0:T(8,128)(2,1)S(1)} %copy-done.5, bf16[320,4096]{1,0:T(8,128)(2,1)S(1)} %copy-done.7), custom_call_target="tpu_custom_call" | custom-call | flops 20971520 | bytes 458752 | tf_op jit(solution)/shard_map/pallas_call | solution.py:243
  224.7 3.3 copy-done
  232.4 28.7 %collective-permute-done.25 = bf16[640,512]{1,0:T(8,128)(2,1)S(1)} collective-permute-done((bf16[640,512]{1,0:T(8,128)(2,1)S(1)}, bf16[640,512]{1,0:T(8,128)(2,1)S(1)}, u32[]{:S(2)}, u32[]{:S(2)}) %collective-permute-start.25) | collective-permute-done | bytes 655392 | tf_op jit(solution)/shard_map/ppermute | solution.py:81
  263.9 31.1 %reduce-scatter.3.cloned.1.call-done = bf16[1024,1024]{1,0:T(8,128)(2,1)} async-done(((bf16[4096,1024]{1,0:T(8,128)(2,1)}), bf16[1024,1024]{1,0:T(8,128)(2,1)}) %reduce-scatter.3.cloned.1.call-update) | async-done | bytes 2097168 | tf_op jit(solution)/shard_map/reduce_scatter | solution.py:460
  301.4 2.4 collective-permute-start.31
  303.8 6.6 %collective-permute-done.30 = bf16[256,512]{1,0:T(8,128)(2,1)S(1)} collective-permute-done((bf16[256,512]{1,0:T(8,128)(2,1)S(1)}, bf16[256,512]{1,0:T(8,128)(2,1)S(1)}, u32[]{:S(2)}, u32[]{:S(2)}) %collective-permute-start.30) | collective-permute-done | bytes 262176 | tf_op jit(solution)/shard_map/ppermute | solution.py:81
  311.6 5.0 %collective-permute-done.31 = bf16[256,512]{1,0:T(8,128)(2,1)S(1)} collective-permute-done((bf16[256,512]{1,0:T(8,128)(2,1)S(1)}, bf16[256,512]{1,0:T(8,128)(2,1)S(1)}, u32[]{:S(2)}, u32[]{:S(2)}) %collective-permute-start.31) | collective-permute-done | bytes 262176 | tf_op jit(solution)/shard_map/ppermute | solution.py:81
  316.6 3.0 collective-permute-done.32
  319.7 3.5 %collective-permute-done.34 = bf16[256,1536]{1,0:T(8,128)(2,1)S(1)} collective-permute-done((bf16[256,1536]{1,0:T(8,128)(2,1)S(1)}, bf16[256,1536]{1,0:T(8,128)(2,1)S(1)}, u32[]{:S(2)}, u32[]{:S(2)}) %collective-permute-start.34) | collective-permute-done | bytes 786464 | tf_op jit(solution)/shard_map/ppermute | solution.py:81
  325.9 3.0 collective-permute-start.41
  (214 shorter events, 87.1 us)
Async XLA Ops:
  7.2 98.6 %all-gather.3.cloned.1.call-start = ((), (), s32[]{:S(2)}) async-start(), calls=%async_computation.2 | async-start | bytes 5242880 | tf_op jit(solution)/shard_map/all_gather | solution.py:455
  9.1 10.6 %collective-permute-start.2 = (bf16[64,1536]{1,0:T(8,128)(2,1)S(1)}, bf16[64,1536]{1,0:T(8,128)(2,1)S(1)}, u32[]{:S(2)}, u32[]{:S(2)}) collective-permute-start(bf16[64,1536]{1,0:T(8,128)(2,1)S(1)} %pad_maximum_fusion.10), channel_id=1, source_target_pairs={{0,1},{1,2},{2,3},{3,0},{4,5},{5,6},{6,7},{7,4},{8,9},{9,10},{10,1... | collective-permute-start | bytes 589832 | tf_op jit(solution)/shard_map/ppermute | solution.py:64
  13.0 15.3 %collective-permute-start.5 = (bf16[64,1664]{1,0:T(8,128)(2,1)S(1)}, bf16[64,1664]{1,0:T(8,128)(2,1)S(1)}, u32[]{:S(2)}, u32[]{:S(2)}) collective-permute-start(bf16[64,1664]{1,0:T(8,128)(2,1)S(1)} %concatenate.43), channel_id=1, source_target_pairs={{0,32},{4,12},{8,40},{12,20},{16,48},{20,28},{24,56},{28,4},{32,64... | collective-permute-start | bytes 638984 | tf_op jit(solution)/shard_map/ppermute | solution.py:64
  14.4 14.0 %collective-permute-start.4 = (bf16[64,1664]{1,0:T(8,128)(2,1)S(1)}, bf16[64,1664]{1,0:T(8,128)(2,1)S(1)}, u32[]{:S(2)}, u32[]{:S(2)}) collective-permute-start(bf16[64,1664]{1,0:T(8,128)(2,1)S(1)} %concatenate.43), channel_id=1, source_target_pairs={{0,64},{4,20},{8,72},{12,28},{16,80},{20,4},{24,88},{28,12},{32,96... | collective-permute-start | bytes 638984 | tf_op jit(solution)/shard_map/ppermute | solution.py:64
  15.0 13.4 %collective-permute-start.3 = (bf16[64,1664]{1,0:T(8,128)(2,1)S(1)}, bf16[64,1664]{1,0:T(8,128)(2,1)S(1)}, u32[]{:S(2)}, u32[]{:S(2)}) collective-permute-start(bf16[64,1664]{1,0:T(8,128)(2,1)S(1)} %concatenate.43), channel_id=1, source_target_pairs={{0,96},{4,28},{8,104},{12,4},{16,112},{20,12},{24,120},{28,20},{32... | collective-permute-start | bytes 638984 | tf_op jit(solution)/shard_map/ppermute | solution.py:64
  28.5 28.7 %collective-permute-start.11 = (bf16[256,1664]{1,0:T(8,128)(2,1)S(1)}, bf16[256,1664]{1,0:T(8,128)(2,1)S(1)}, u32[]{:S(2)}, u32[]{:S(2)}) collective-permute-start(bf16[256,1664]{1,0:T(8,128)(2,1)S(1)} %constant_dynamic-update-slice_fusion.refs_0_), channel_id=1, source_target_pairs={{0,8},{4,36},{8,16},{12,44},{16,24},{20,52},{24,0},{28,60},{32,40}... | collective-permute-start | bytes 2555912 | tf_op jit(solution)/shard_map/ppermute | solution.py:64
  30.6 26.6 %collective-permute-start.10 = (bf16[256,1664]{1,0:T(8,128)(2,1)S(1)}, bf16[256,1664]{1,0:T(8,128)(2,1)S(1)}, u32[]{:S(2)}, u32[]{:S(2)}) collective-permute-start(bf16[256,1664]{1,0:T(8,128)(2,1)S(1)} %constant_dynamic-update-slice_fusion.refs_0_), channel_id=1, source_target_pairs={{0,16},{4,68},{8,24},{12,76},{16,0},{20,84},{24,8},{28,92},{32,48}... | collective-permute-start | bytes 2555912 | tf_op jit(solution)/shard_map/ppermute | solution.py:64
  31.7 26.4 %collective-permute-start.9 = (bf16[256,1664]{1,0:T(8,128)(2,1)S(1)}, bf16[256,1664]{1,0:T(8,128)(2,1)S(1)}, u32[]{:S(2)}, u32[]{:S(2)}) collective-permute-start(bf16[256,1664]{1,0:T(8,128)(2,1)S(1)} %constant_dynamic-update-slice_fusion.refs_0_), channel_id=1, source_target_pairs={{0,24},{4,100},{8,0},{12,108},{16,8},{20,116},{24,16},{28,124},{32... | collective-permute-start | bytes 2555912 | tf_op jit(solution)/shard_map/ppermute | solution.py:64
  34.8 13.5 %collective-permute-start.7 = (bf16[256,512]{1,0:T(8,128)(2,1)S(1)}, bf16[256,512]{1,0:T(8,128)(2,1)S(1)}, u32[]{:S(2)}, u32[]{:S(2)}) collective-permute-start(bf16[256,512]{1,0:T(8,128)(2,1)S(1)} %pad_maximum_fusion.9), channel_id=1, source_target_pairs={{0,64},{4,20},{8,72},{12,28},{16,80},{20,4},{24,88},{28,12},{32,96... | collective-permute-start | bytes 786440 | tf_op jit(solution)/shard_map/ppermute | solution.py:64
  60.1 108.2 %all-gather.5.cloned.1.call-start = ((), (), s32[]{:S(2)}) async-start(), calls=%async_computation.3 | async-start | bytes 10485760 | tf_op jit(solution)/shard_map/all_gather | solution.py:455
  65.4 10.0 %collective-permute-start.16 = (bf16[256,1024]{1,0:T(8,128)(2,1)S(1)}, bf16[256,1024]{1,0:T(8,128)(2,1)S(1)}, u32[]{:S(2)}, u32[]{:S(2)}) collective-permute-start(bf16[256,1024]{1,0:T(8,128)(2,1)S(1)} %pad_maximum_fusion.8), channel_id=1, source_target_pairs={{0,32},{4,12},{8,40},{12,20},{16,48},{20,28},{24,56},{28,4},{32,64... | collective-permute-start | bytes 1572872 | tf_op jit(solution)/shard_map/ppermute | solution.py:64
  68.1 33.4 %collective-permute-start.19 = (bf16[640,512]{1,0:T(8,128)(2,1)S(1)}, bf16[640,512]{1,0:T(8,128)(2,1)S(1)}, u32[]{:S(2)}, u32[]{:S(2)}) collective-permute-start(bf16[640,512]{1,0:T(8,128)(2,1)S(1)} %pad_maximum_fusion.7.refs_0_), channel_id=1, source_target_pairs={{0,1},{1,2},{2,3},{3,0},{4,5},{5,6},{6,7},{7,4},{8,9},{9,10},{10,1... | collective-permute-start | bytes 1966088 | tf_op jit(solution)/shard_map/ppermute | solution.py:64
  70.6 31.9 %collective-permute-start.18 = (bf16[640,512]{1,0:T(8,128)(2,1)S(1)}, bf16[640,512]{1,0:T(8,128)(2,1)S(1)}, u32[]{:S(2)}, u32[]{:S(2)}) collective-permute-start(bf16[640,512]{1,0:T(8,128)(2,1)S(1)} %pad_maximum_fusion.7.refs_0_), channel_id=1, source_target_pairs={{0,2},{1,3},{2,0},{3,1},{4,6},{5,7},{6,4},{7,5},{8,10},{9,11},{10,... | collective-permute-start | bytes 1966088 | tf_op jit(solution)/shard_map/ppermute | solution.py:64
  73.0 30.4 %collective-permute-start.17 = (bf16[640,512]{1,0:T(8,128)(2,1)S(1)}, bf16[640,512]{1,0:T(8,128)(2,1)S(1)}, u32[]{:S(2)}, u32[]{:S(2)}) collective-permute-start(bf16[640,512]{1,0:T(8,128)(2,1)S(1)} %pad_maximum_fusion.7.refs_0_), channel_id=1, source_target_pairs={{0,3},{1,0},{2,1},{3,2},{4,7},{5,4},{6,5},{7,6},{8,11},{9,8},{10,9... | collective-permute-start | bytes 1966088 | tf_op jit(solution)/shard_map/ppermute | solution.py:64
  74.3 16.3 %collective-permute-start.15 = (bf16[256,1024]{1,0:T(8,128)(2,1)S(1)}, bf16[256,1024]{1,0:T(8,128)(2,1)S(1)}, u32[]{:S(2)}, u32[]{:S(2)}) collective-permute-start(bf16[256,1024]{1,0:T(8,128)(2,1)S(1)} %pad_maximum_fusion.8), channel_id=1, source_target_pairs={{0,64},{4,20},{8,72},{12,28},{16,80},{20,4},{24,88},{28,12},{32,96... | collective-permute-start | bytes 1572872 | tf_op jit(solution)/shard_map/ppermute | solution.py:64
  75.4 26.2 %collective-permute-start.14 = (bf16[256,1024]{1,0:T(8,128)(2,1)S(1)}, bf16[256,1024]{1,0:T(8,128)(2,1)S(1)}, u32[]{:S(2)}, u32[]{:S(2)}) collective-permute-start(bf16[256,1024]{1,0:T(8,128)(2,1)S(1)} %pad_maximum_fusion.8), channel_id=1, source_target_pairs={{0,96},{4,28},{8,104},{12,4},{16,112},{20,12},{24,120},{28,20},{32... | collective-permute-start | bytes 1572872 | tf_op jit(solution)/shard_map/ppermute | solution.py:64
  108.8 155.1 %reduce-scatter.5.cloned.1.call-start = ((), (), s32[]{:S(2)}) async-start(), calls=%async_computation.5 | async-start | bytes 5242880 | tf_op jit(solution)/shard_map/reduce_scatter | solution.py:460
  109.1 18.9 %collective-permute-start.13 = (bf16[640,1024]{1,0:T(8,128)(2,1)S(1)}, bf16[640,1024]{1,0:T(8,128)(2,1)S(1)}, u32[]{:S(2)}, u32[]{:S(2)}) collective-permute-start(bf16[640,1024]{1,0:T(8,128)(2,1)S(1)} %pad_maximum_fusion.1.refs_0_), channel_id=1, source_target_pairs={{0,1},{1,2},{2,3},{3,0},{4,7},{5,4},{6,5},{7,6},{8,9},{9,10},{10,1... | collective-permute-start | bytes 3932168 | tf_op jit(solution)/shard_map/ppermute | solution.py:75
  113.5 14.5 %collective-permute-start.20 = (bf16[320,2048]{1,0:T(8,128)(2,1)S(1)}, bf16[320,2048]{1,0:T(8,128)(2,1)S(1)}, u32[]{:S(2)}, u32[]{:S(2)}) collective-permute-start(bf16[320,2048]{1,0:T(8,128)(2,1)S(1)} %get-tuple-element.107), channel_id=1, source_target_pairs={{0,4},{4,0},{8,12},{12,8},{16,20},{20,16},{24,28},{28,24},{32,36},... | collective-permute-start | bytes 3932168 | tf_op jit(solution)/shard_map/ppermute | solution.py:92
  128.0 18.8 %collective-permute-start.21 = (bf16[640,1024]{1,0:T(8,128)(2,1)S(1)}, bf16[640,1024]{1,0:T(8,128)(2,1)S(1)}, u32[]{:S(2)}, u32[]{:S(2)}) collective-permute-start(bf16[640,1024]{1,0:T(8,128)(2,1)S(1)} %collective-permute-done.13.refs_1_), channel_id=1, source_target_pairs={{0,1},{1,2},{2,3},{3,0},{4,7},{5,4},{6,5},{7,6},{8,9},{9,10},{10,1... | collective-permute-start | bytes 3932168 | tf_op jit(solution)/shard_map/ppermute | solution.py:75
  146.8 20.0 %collective-permute-start.23 = (bf16[320,4096]{1,0:T(8,128)(2,1)S(1)}, bf16[320,4096]{1,0:T(8,128)(2,1)S(1)}, u32[]{:S(2)}, u32[]{:S(2)}) collective-permute-start(bf16[320,4096]{1,0:T(8,128)(2,1)S(1)} %get-tuple-element.121), channel_id=1, source_target_pairs={{0,4},{4,0},{8,12},{12,8},{16,20},{20,16},{24,28},{28,24},{32,36},... | collective-permute-start | bytes 7864328 | tf_op jit(solution)/shard_map/ppermute | solution.py:92
  146.8 18.8 %collective-permute-start.22 = (bf16[640,1024]{1,0:T(8,128)(2,1)S(1)}, bf16[640,1024]{1,0:T(8,128)(2,1)S(1)}, u32[]{:S(2)}, u32[]{:S(2)}) collective-permute-start(bf16[640,1024]{1,0:T(8,128)(2,1)S(1)} %collective-permute-done.21.refs_2_), channel_id=1, source_target_pairs={{0,1},{1,2},{2,3},{3,0},{4,7},{5,4},{6,5},{7,6},{8,9},{9,10},{10,1... | collective-permute-start | bytes 3932168 | tf_op jit(solution)/shard_map/ppermute | solution.py:75
  216.7 78.3 %reduce-scatter.3.cloned.1.call-start = ((), (), s32[]{:S(2)}) async-start(), calls=%async_computation.4 | async-start | bytes 10485760 | tf_op jit(solution)/shard_map/reduce_scatter | solution.py:460
  229.1 32.0 %collective-permute-start.25 = (bf16[640,512]{1,0:T(8,128)(2,1)S(1)}, bf16[640,512]{1,0:T(8,128)(2,1)S(1)}, u32[]{:S(2)}, u32[]{:S(2)}) collective-permute-start(bf16[640,512]{1,0:T(8,128)(2,1)S(1)} %copy-done.27), channel_id=1, source_target_pairs={{0,1},{1,2},{2,3},{3,0},{4,5},{5,6},{6,7},{7,4},{8,9},{9,10},{10,1... | collective-permute-start | bytes 1966088 | tf_op jit(solution)/shard_map/ppermute | solution.py:81
  229.3 31.9 %collective-permute-start.26 = (bf16[640,512]{1,0:T(8,128)(2,1)S(1)}, bf16[640,512]{1,0:T(8,128)(2,1)S(1)}, u32[]{:S(2)}, u32[]{:S(2)}) collective-permute-start(bf16[640,512]{1,0:T(8,128)(2,1)S(1)} %copy-done.25), channel_id=1, source_target_pairs={{0,2},{1,3},{2,0},{3,1},{4,6},{5,7},{6,4},{7,5},{8,10},{9,11},{10,... | collective-permute-start | bytes 1966088 | tf_op jit(solution)/shard_map/ppermute | solution.py:81
  231.1 30.7 %collective-permute-start.27 = (bf16[640,512]{1,0:T(8,128)(2,1)S(1)}, bf16[640,512]{1,0:T(8,128)(2,1)S(1)}, u32[]{:S(2)}, u32[]{:S(2)}) collective-permute-start(bf16[640,512]{1,0:T(8,128)(2,1)S(1)} %copy-done.23), channel_id=1, source_target_pairs={{0,3},{1,0},{2,1},{3,2},{4,7},{5,4},{6,5},{7,6},{8,11},{9,8},{10,9... | collective-permute-start | bytes 1966088 | tf_op jit(solution)/shard_map/ppermute | solution.py:81
  297.1 22.6 %collective-permute-start.33 = (bf16[256,1536]{1,0:T(8,128)(2,1)S(1)}, bf16[256,1536]{1,0:T(8,128)(2,1)S(1)}, u32[]{:S(2)}, u32[]{:S(2)}) collective-permute-start(bf16[256,1536]{1,0:T(8,128)(2,1)S(1)} %pad_maximum_fusion.4), channel_id=1, source_target_pairs={{0,32},{4,12},{8,40},{12,20},{16,48},{20,28},{24,56},{28,4},{32,64... | collective-permute-start | bytes 2359304 | tf_op jit(solution)/shard_map/ppermute | solution.py:81
  298.4 24.8 %collective-permute-start.34 = (bf16[256,1536]{1,0:T(8,128)(2,1)S(1)}, bf16[256,1536]{1,0:T(8,128)(2,1)S(1)}, u32[]{:S(2)}, u32[]{:S(2)}) collective-permute-start(bf16[256,1536]{1,0:T(8,128)(2,1)S(1)} %pad_maximum_fusion.5), channel_id=1, source_target_pairs={{0,64},{4,20},{8,72},{12,28},{16,80},{20,4},{24,88},{28,12},{32,96... | collective-permute-start | bytes 2359304 | tf_op jit(solution)/shard_map/ppermute | solution.py:81
  299.4 26.1 %collective-permute-start.35 = (bf16[256,1536]{1,0:T(8,128)(2,1)S(1)}, bf16[256,1536]{1,0:T(8,128)(2,1)S(1)}, u32[]{:S(2)}, u32[]{:S(2)}) collective-permute-start(bf16[256,1536]{1,0:T(8,128)(2,1)S(1)} %pad_maximum_fusion.6), channel_id=1, source_target_pairs={{0,96},{4,28},{8,104},{12,4},{16,112},{20,12},{24,120},{28,20},{32... | collective-permute-start | bytes 2359304 | tf_op jit(solution)/shard_map/ppermute | solution.py:81
  301.4 15.3 %collective-permute-start.31 = (bf16[256,512]{1,0:T(8,128)(2,1)S(1)}, bf16[256,512]{1,0:T(8,128)(2,1)S(1)}, u32[]{:S(2)}, u32[]{:S(2)}) collective-permute-start(bf16[256,512]{1,0:T(8,128)(2,1)S(1)} %get-tuple-element.150), channel_id=1, source_target_pairs={{0,16},{4,68},{8,24},{12,76},{16,0},{20,84},{24,8},{28,92},{32,48}... | collective-permute-start | bytes 786440 | tf_op jit(solution)/shard_map/ppermute | solution.py:81
  325.9 13.4 %collective-permute-start.41 = (bf16[64,1536]{1,0:T(8,128)(2,1)S(1)}, bf16[64,1536]{1,0:T(8,128)(2,1)S(1)}, u32[]{:S(2)}, u32[]{:S(2)}) collective-permute-start(bf16[64,1536]{1,0:T(8,128)(2,1)S(1)} %get-tuple-element.178), channel_id=1, source_target_pairs={{0,3},{1,0},{2,1},{3,2},{4,7},{5,4},{6,5},{7,6},{8,11},{9,8},{10,9... | collective-permute-start | bytes 589832 | tf_op jit(solution)/shard_map/ppermute | solution.py:81
  328.9 10.4 %collective-permute-start.40 = (bf16[64,1536]{1,0:T(8,128)(2,1)S(1)}, bf16[64,1536]{1,0:T(8,128)(2,1)S(1)}, u32[]{:S(2)}, u32[]{:S(2)}) collective-permute-start(bf16[64,1536]{1,0:T(8,128)(2,1)S(1)} %get-tuple-element.179), channel_id=1, source_target_pairs={{0,2},{1,3},{2,0},{3,1},{4,6},{5,7},{6,4},{7,5},{8,10},{9,11},{10,... | collective-permute-start | bytes 589832 | tf_op jit(solution)/shard_map/ppermute | solution.py:81
  (60 other events, 400.9 us)
Sparse Core Ops, SparseCore 0:
  60.2 45.4 all-gather.2
  108.9 50.2 all-gather.4
  216.8 28.6 reduce-scatter.4
  248.0 46.9 reduce-scatter.2

commit v4 on v3

--- a/solution.py
+++ b/solution.py
@@ -492,9 +492,10 @@
     near_b += around(near_b[2], 1)[1:]
     near_b, sibling_a, dense_b = together(near_b, swap(sibling_a), dense_b)
 
-    group_a = scatter_section(scatter_last(where, slots_a, own_a, sibling_a))
+    dense_a = scatter_last(where, slots_a, own_a, sibling_a)
     own, sibling = gather_last(where, slots_b, dense_b)
-    sibling = swap(sibling)
+    sibling, dense_a = together(swap(sibling), dense_a)
+    group_a = scatter_section(dense_a)
     *near_b, own_b, sibling_b = expert_call(
         True, where, near_b, (own, sibling), rows, w_gate, w_up, w_down
     )

time: 350 us -> 352 us (level)
  local copies, waits for them, and re-layouts: 38.1 us -> 31.9 us
  waiting for transfers between devices: 184 us -> 190 us
    reduce_scatter x2, waiting for transfers between devices: 31.1 us -> 42.2 us  [scatter_section(): lax.psum_scatter(dense, 'section', scatter_dimension=0, tiled=True, axis_...]
    unnamed x89 -> x87, local copies, waits for them, and re-layouts: 33.1 us -> 26.9 us
    ppermute x6, waiting for transfers between devices: 11.1 us -> 5.92 us  [swap(): return lax.ppermute(values, 'section', SWAP)]
  transfers between devices with their start and end apart: 46 -> 46, of which waited for: 27 -> 26; matrix products, arithmetic and copies ran while one was open for 1% -> 1% of each run, Pallas kernels for 7% -> 7%
where the time goes in v4:
time: 352 us; the launch traced here: 349 us
  waiting for transfers between devices  190 us (54%)
  Pallas kernels  54.6 us (16%)
  starting transfers between devices  50.2 us (14%)
  local copies, waits for them, and re-layouts  31.9 us (9%)
  between operations  14.4 us (4%)
  other arithmetic  7.66 us (2%)
    ppermute x18, waiting for transfers between devices, spread(): lax.ppermute(values, axis, shifts[4 - d])  53.6 us
    ppermute x15, waiting for transfers between devices, send(): lax.ppermute(parts[d], axis, shifts[d])  53 us
    reduce_scatter x2, waiting for transfers between devices, scatter_section(): lax.psum_scatter(dense, 'section', scatter_dimension=0, tiled=True, axis_...  42.2 us
    pallas_call x2, Pallas kernels, expert_call(): pl.pallas_call(backward_kernel if backward else forward_kernel, grid_spec...  37.8 us
    ppermute x3, waiting for transfers between devices, around(): parts.append(lax.ppermute(parts[-1], ('section', 'expert'), DEPTH_RING))  33.7 us
    unnamed x87, local copies, waits for them, and re-layouts  26.9 us
    ppermute x18, starting transfers between devices, spread(): lax.ppermute(values, axis, shifts[4 - d])  26.8 us
    ppermute x15, starting transfers between devices, send(): lax.ppermute(parts[d], axis, shifts[d])  20.6 us
  transfers between devices with their start and end apart: 46, of which 26 were waited for; matrix products, arithmetic and copies ran while one was open for 1% of the time, Pallas kernels for 7%

profile of v4, /device:TPU:16, one launch (start us, length us, event | category | flops | bytes accessed | tf_op | source)
XLA Modules:
  0.0 349.2 jit_solution(2542242402334192868)
XLA Ops:
  16.1 3.6 %collective-permute-start.1 = (bf16[64,1536]{1,0:T(8,128)(2,1)S(1)}, bf16[64,1536]{1,0:T(8,128)(2,1)S(1)}, u32[]{:S(2)}, u32[]{:S(2)}) collective-permute-start(bf16[64,1536]{1,0:T(8,128)(2,1)S(1)} %pad_maximum_fusion.10), channel_id=1, source_target_pairs={{0,2},{1,3},{2,0},{3,1},{4,6},{5,7},{6,4},{7,5},{8,10},{9,11},{10,... | collective-permute-start | bytes 589832 | tf_op jit(solution)/shard_map/ppermute | solution.py:64
  20.7 4.1 %collective-permute-done.1 = bf16[64,1536]{1,0:T(8,128)(2,1)S(1)} collective-permute-done((bf16[64,1536]{1,0:T(8,128)(2,1)S(1)}, bf16[64,1536]{1,0:T(8,128)(2,1)S(1)}, u32[]{:S(2)}, u32[]{:S(2)}) %collective-permute-start.1) | collective-permute-done | bytes 196640 | tf_op jit(solution)/shard_map/ppermute | solution.py:64
  24.7 3.6 %collective-permute-done = bf16[64,1536]{1,0:T(8,128)(2,1)S(1)} collective-permute-done((bf16[64,1536]{1,0:T(8,128)(2,1)S(1)}, bf16[64,1536]{1,0:T(8,128)(2,1)S(1)}, u32[]{:S(2)}, u32[]{:S(2)}) %collective-permute-start) | collective-permute-done | bytes 196640 | tf_op jit(solution)/shard_map/ppermute | solution.py:64
  35.4 7.5 %collective-permute-done.8 = bf16[256,512]{1,0:T(8,128)(2,1)S(1)} collective-permute-done((bf16[256,512]{1,0:T(8,128)(2,1)S(1)}, bf16[256,512]{1,0:T(8,128)(2,1)S(1)}, u32[]{:S(2)}, u32[]{:S(2)}) %collective-permute-start.8) | collective-permute-done | bytes 262176 | tf_op jit(solution)/shard_map/ppermute | solution.py:64
  43.1 5.2 %collective-permute-done.7 = bf16[256,512]{1,0:T(8,128)(2,1)S(1)} collective-permute-done((bf16[256,512]{1,0:T(8,128)(2,1)S(1)}, bf16[256,512]{1,0:T(8,128)(2,1)S(1)}, u32[]{:S(2)}, u32[]{:S(2)}) %collective-permute-start.7) | collective-permute-done | bytes 262176 | tf_op jit(solution)/shard_map/ppermute | solution.py:64
  48.3 3.8 %collective-permute-done.6 = bf16[256,512]{1,0:T(8,128)(2,1)S(1)} collective-permute-done((bf16[256,512]{1,0:T(8,128)(2,1)S(1)}, bf16[256,512]{1,0:T(8,128)(2,1)S(1)}, u32[]{:S(2)}, u32[]{:S(2)}) %collective-permute-start.6) | collective-permute-done | bytes 262176 | tf_op jit(solution)/shard_map/ppermute | solution.py:64
  52.1 5.1 %collective-permute-done.11.refs_3_ = bf16[256,1664]{1,0:T(8,128)(2,1)S(1)} collective-permute-done((bf16[256,1664]{1,0:T(8,128)(2,1)S(1)}, bf16[256,1664]{1,0:T(8,128)(2,1)S(1)}, u32[]{:S(2)}, u32[]{:S(2)}) %collective-permute-start.11) | collective-permute-done | bytes 852000 | tf_op jit(solution)/shard_map/ppermute | solution.py:64
  62.6 2.5 shard_map.113
  68.2 2.4 collective-permute-start.19
  70.6 2.4 collective-permute-start.18
  77.3 13.3 %collective-permute-done.15 = bf16[256,1024]{1,0:T(8,128)(2,1)S(1)} collective-permute-done((bf16[256,1024]{1,0:T(8,128)(2,1)S(1)}, bf16[256,1024]{1,0:T(8,128)(2,1)S(1)}, u32[]{:S(2)}, u32[]{:S(2)}) %collective-permute-start.15) | collective-permute-done | bytes 524320 | tf_op jit(solution)/shard_map/ppermute | solution.py:64
  90.6 11.0 %collective-permute-done.14 = bf16[256,1024]{1,0:T(8,128)(2,1)S(1)} collective-permute-done((bf16[256,1024]{1,0:T(8,128)(2,1)S(1)}, bf16[256,1024]{1,0:T(8,128)(2,1)S(1)}, u32[]{:S(2)}, u32[]{:S(2)}) %collective-permute-start.14) | collective-permute-done | bytes 524320 | tf_op jit(solution)/shard_map/ppermute | solution.py:64
  105.7 3.0 pad_maximum_fusion
  113.6 14.4 %collective-permute-done.13.refs_1_ = bf16[640,1024]{1,0:T(8,128)(2,1)S(1)} collective-permute-done((bf16[640,1024]{1,0:T(8,128)(2,1)S(1)}, bf16[640,1024]{1,0:T(8,128)(2,1)S(1)}, u32[]{:S(2)}, u32[]{:S(2)}) %collective-permute-start.13) | collective-permute-done | bytes 1310752 | tf_op jit(solution)/shard_map/ppermute | solution.py:75
  128.3 15.4 %shard_map.115 = (bf16[320,4096]{1,0:T(8,128)(2,1)S(1)}, bf16[320,4096]{1,0:T(8,128)(2,1)S(1)}) custom-call(s32[5]{0:T(128)S(1)} %stack.23.where, bf16[640,512]{1,0:T(8,128)(2,1)S(1)} %pad_maximum_fusion.7.refs_0_, bf16[640,512]{1,0:T(8,128)(2,1)S(1)} %copy-done.21, bf16[640,512]{1,0:T(8,128)(2,1)S(1)} %copy-done.19, bf16[640,512]{1,0:T(8,128)(2,1)S(1)} %copy-done.17, ...), custom_call_target="tpu_custom_call" | custom-call | flops 125829120 | bytes 491520 | tf_op jit(solution)/shard_map/pallas_call | solution.py:414
  147.9 17.7 %collective-permute-done.22.refs_3_ = bf16[640,1024]{1,0:T(8,128)(2,1)S(1)} collective-permute-done((bf16[640,1024]{1,0:T(8,128)(2,1)S(1)}, bf16[640,1024]{1,0:T(8,128)(2,1)S(1)}, u32[]{:S(2)}, u32[]{:S(2)}) %collective-permute-start.22) | collective-permute-done | bytes 1310752 | tf_op jit(solution)/shard_map/ppermute | solution.py:75
  168.2 3.4 copy-done.2
  171.6 5.7 %shard_map.116 = (bf16[320,4096]{1,0:T(8,128)(2,1)S(1)}, bf16[320,4096]{1,0:T(8,128)(2,1)}) custom-call(s32[5]{0:T(128)S(1)} %stack.23.where, bf16[4,160,256]{2,1,0:T(8,128)(2,1)S(1)} %get-tuple-element.100.slots_ref, bf16[4096,1024]{1,0:T(8,128)(2,1)S(1)} %copy-done.2), custom_call_target="tpu_custom_call" | custom-call | flops 20971520 | bytes 458752 | tf_op jit(solution)/shard_map/pallas_call | solution.py:193
  178.9 3.6 %shard_map.117 = bf16[4096,1024]{1,0:T(8,128)(2,1)S(1)} custom-call(s32[5]{0:T(128)S(1)} %stack.23.where, bf16[4,160,256]{2,1,0:T(8,128)(2,1)S(1)} %copy-done.11, bf16[320,4096]{1,0:T(8,128)(2,1)S(1)} %copy-done.5, bf16[320,4096]{1,0:T(8,128)(2,1)S(1)} %copy-done.7), custom_call_target="tpu_custom_call" | custom-call | flops 20971520 | bytes 458752 | tf_op jit(solution)/shard_map/pallas_call | solution.py:243
  182.4 3.3 copy-done
  185.8 22.4 %shard_map.118 = (bf16[640,512]{1,0:T(8,128)(2,1)S(1)}, bf16[640,512]{1,0:T(8,128)(2,1)S(1)}, bf16[640,512]{1,0:T(8,128)(2,1)S(1)}, bf16[640,512]{1,0:T(8,128)(2...) custom-call(s32[5]{0:T(128)S(1)} %stack.23.where, bf16[640,1024]{1,0:T(8,128)(2,1)} %copy-done.28, ...), custom_call_target="tpu_custom_call" | custom-call | flops 209715200 | bytes 491520 | tf_op jit(solution)/shard_map/pallas_call | solution.py:414
  211.2 2.7 collective-permute-done.29.sibling_ref
  213.9 2.5 shard_map.119
  222.9 28.9 %collective-permute-done.25 = bf16[640,512]{1,0:T(8,128)(2,1)S(1)} collective-permute-done((bf16[640,512]{1,0:T(8,128)(2,1)S(1)}, bf16[640,512]{1,0:T(8,128)(2,1)S(1)}, u32[]{:S(2)}, u32[]{:S(2)}) %collective-permute-start.25) | collective-permute-done | bytes 655392 | tf_op jit(solution)/shard_map/ppermute | solution.py:81
  254.6 42.2 %reduce-scatter.3.cloned.1.call-done = bf16[1024,1024]{1,0:T(8,128)(2,1)} async-done(((bf16[4096,1024]{1,0:T(8,128)(2,1)}), bf16[1024,1024]{1,0:T(8,128)(2,1)}) %reduce-scatter.3.cloned.1.call-update) | async-done | bytes 2097168 | tf_op jit(solution)/shard_map/reduce_scatter | solution.py:460
  303.2 2.4 collective-permute-start.31
  305.7 6.6 %collective-permute-done.30 = bf16[256,512]{1,0:T(8,128)(2,1)S(1)} collective-permute-done((bf16[256,512]{1,0:T(8,128)(2,1)S(1)}, bf16[256,512]{1,0:T(8,128)(2,1)S(1)}, u32[]{:S(2)}, u32[]{:S(2)}) %collective-permute-start.30) | collective-permute-done | bytes 262176 | tf_op jit(solution)/shard_map/ppermute | solution.py:81
  313.5 5.0 %collective-permute-done.31 = bf16[256,512]{1,0:T(8,128)(2,1)S(1)} collective-permute-done((bf16[256,512]{1,0:T(8,128)(2,1)S(1)}, bf16[256,512]{1,0:T(8,128)(2,1)S(1)}, u32[]{:S(2)}, u32[]{:S(2)}) %collective-permute-start.31) | collective-permute-done | bytes 262176 | tf_op jit(solution)/shard_map/ppermute | solution.py:81
  318.5 3.0 collective-permute-done.32
  321.5 3.6 %collective-permute-done.34 = bf16[256,1536]{1,0:T(8,128)(2,1)S(1)} collective-permute-done((bf16[256,1536]{1,0:T(8,128)(2,1)S(1)}, bf16[256,1536]{1,0:T(8,128)(2,1)S(1)}, u32[]{:S(2)}, u32[]{:S(2)}) %collective-permute-start.34) | collective-permute-done | bytes 786464 | tf_op jit(solution)/shard_map/ppermute | solution.py:81
  327.8 3.0 collective-permute-start.41
  336.9 2.3 collective-permute-start.36
  (212 shorter events, 79.1 us)
Async XLA Ops:
  7.2 98.6 %all-gather.3.cloned.1.call-start = ((), (), s32[]{:S(2)}) async-start(), calls=%async_computation.2 | async-start | bytes 5242880 | tf_op jit(solution)/shard_map/all_gather | solution.py:455
  9.1 10.6 %collective-permute-start.2 = (bf16[64,1536]{1,0:T(8,128)(2,1)S(1)}, bf16[64,1536]{1,0:T(8,128)(2,1)S(1)}, u32[]{:S(2)}, u32[]{:S(2)}) collective-permute-start(bf16[64,1536]{1,0:T(8,128)(2,1)S(1)} %pad_maximum_fusion.10), channel_id=1, source_target_pairs={{0,1},{1,2},{2,3},{3,0},{4,5},{5,6},{6,7},{7,4},{8,9},{9,10},{10,1... | collective-permute-start | bytes 589832 | tf_op jit(solution)/shard_map/ppermute | solution.py:64
  13.0 15.3 %collective-permute-start.5 = (bf16[64,1664]{1,0:T(8,128)(2,1)S(1)}, bf16[64,1664]{1,0:T(8,128)(2,1)S(1)}, u32[]{:S(2)}, u32[]{:S(2)}) collective-permute-start(bf16[64,1664]{1,0:T(8,128)(2,1)S(1)} %concatenate.43), channel_id=1, source_target_pairs={{0,32},{4,12},{8,40},{12,20},{16,48},{20,28},{24,56},{28,4},{32,64... | collective-permute-start | bytes 638984 | tf_op jit(solution)/shard_map/ppermute | solution.py:64
  14.4 14.0 %collective-permute-start.4 = (bf16[64,1664]{1,0:T(8,128)(2,1)S(1)}, bf16[64,1664]{1,0:T(8,128)(2,1)S(1)}, u32[]{:S(2)}, u32[]{:S(2)}) collective-permute-start(bf16[64,1664]{1,0:T(8,128)(2,1)S(1)} %concatenate.43), channel_id=1, source_target_pairs={{0,64},{4,20},{8,72},{12,28},{16,80},{20,4},{24,88},{28,12},{32,96... | collective-permute-start | bytes 638984 | tf_op jit(solution)/shard_map/ppermute | solution.py:64
  15.0 13.4 %collective-permute-start.3 = (bf16[64,1664]{1,0:T(8,128)(2,1)S(1)}, bf16[64,1664]{1,0:T(8,128)(2,1)S(1)}, u32[]{:S(2)}, u32[]{:S(2)}) collective-permute-start(bf16[64,1664]{1,0:T(8,128)(2,1)S(1)} %concatenate.43), channel_id=1, source_target_pairs={{0,96},{4,28},{8,104},{12,4},{16,112},{20,12},{24,120},{28,20},{32... | collective-permute-start | bytes 638984 | tf_op jit(solution)/shard_map/ppermute | solution.py:64
  28.5 28.7 %collective-permute-start.11 = (bf16[256,1664]{1,0:T(8,128)(2,1)S(1)}, bf16[256,1664]{1,0:T(8,128)(2,1)S(1)}, u32[]{:S(2)}, u32[]{:S(2)}) collective-permute-start(bf16[256,1664]{1,0:T(8,128)(2,1)S(1)} %constant_dynamic-update-slice_fusion.refs_0_), channel_id=1, source_target_pairs={{0,8},{4,36},{8,16},{12,44},{16,24},{20,52},{24,0},{28,60},{32,40}... | collective-permute-start | bytes 2555912 | tf_op jit(solution)/shard_map/ppermute | solution.py:64
  30.6 26.6 %collective-permute-start.10 = (bf16[256,1664]{1,0:T(8,128)(2,1)S(1)}, bf16[256,1664]{1,0:T(8,128)(2,1)S(1)}, u32[]{:S(2)}, u32[]{:S(2)}) collective-permute-start(bf16[256,1664]{1,0:T(8,128)(2,1)S(1)} %constant_dynamic-update-slice_fusion.refs_0_), channel_id=1, source_target_pairs={{0,16},{4,68},{8,24},{12,76},{16,0},{20,84},{24,8},{28,92},{32,48}... | collective-permute-start | bytes 2555912 | tf_op jit(solution)/shard_map/ppermute | solution.py:64
  31.7 26.5 %collective-permute-start.9 = (bf16[256,1664]{1,0:T(8,128)(2,1)S(1)}, bf16[256,1664]{1,0:T(8,128)(2,1)S(1)}, u32[]{:S(2)}, u32[]{:S(2)}) collective-permute-start(bf16[256,1664]{1,0:T(8,128)(2,1)S(1)} %constant_dynamic-update-slice_fusion.refs_0_), channel_id=1, source_target_pairs={{0,24},{4,100},{8,0},{12,108},{16,8},{20,116},{24,16},{28,124},{32... | collective-permute-start | bytes 2555912 | tf_op jit(solution)/shard_map/ppermute | solution.py:64
  34.8 13.5 %collective-permute-start.7 = (bf16[256,512]{1,0:T(8,128)(2,1)S(1)}, bf16[256,512]{1,0:T(8,128)(2,1)S(1)}, u32[]{:S(2)}, u32[]{:S(2)}) collective-permute-start(bf16[256,512]{1,0:T(8,128)(2,1)S(1)} %pad_maximum_fusion.9), channel_id=1, source_target_pairs={{0,64},{4,20},{8,72},{12,28},{16,80},{20,4},{24,88},{28,12},{32,96... | collective-permute-start | bytes 786440 | tf_op jit(solution)/shard_map/ppermute | solution.py:64
  60.1 108.1 %all-gather.5.cloned.1.call-start = ((), (), s32[]{:S(2)}) async-start(), calls=%async_computation.3 | async-start | bytes 10485760 | tf_op jit(solution)/shard_map/all_gather | solution.py:455
  65.4 10.0 %collective-permute-start.16 = (bf16[256,1024]{1,0:T(8,128)(2,1)S(1)}, bf16[256,1024]{1,0:T(8,128)(2,1)S(1)}, u32[]{:S(2)}, u32[]{:S(2)}) collective-permute-start(bf16[256,1024]{1,0:T(8,128)(2,1)S(1)} %pad_maximum_fusion.8), channel_id=1, source_target_pairs={{0,32},{4,12},{8,40},{12,20},{16,48},{20,28},{24,56},{28,4},{32,64... | collective-permute-start | bytes 1572872 | tf_op jit(solution)/shard_map/ppermute | solution.py:64
  68.2 33.4 %collective-permute-start.19 = (bf16[640,512]{1,0:T(8,128)(2,1)S(1)}, bf16[640,512]{1,0:T(8,128)(2,1)S(1)}, u32[]{:S(2)}, u32[]{:S(2)}) collective-permute-start(bf16[640,512]{1,0:T(8,128)(2,1)S(1)} %pad_maximum_fusion.7.refs_0_), channel_id=1, source_target_pairs={{0,1},{1,2},{2,3},{3,0},{4,5},{5,6},{6,7},{7,4},{8,9},{9,10},{10,1... | collective-permute-start | bytes 1966088 | tf_op jit(solution)/shard_map/ppermute | solution.py:64
  70.6 31.9 %collective-permute-start.18 = (bf16[640,512]{1,0:T(8,128)(2,1)S(1)}, bf16[640,512]{1,0:T(8,128)(2,1)S(1)}, u32[]{:S(2)}, u32[]{:S(2)}) collective-permute-start(bf16[640,512]{1,0:T(8,128)(2,1)S(1)} %pad_maximum_fusion.7.refs_0_), channel_id=1, source_target_pairs={{0,2},{1,3},{2,0},{3,1},{4,6},{5,7},{6,4},{7,5},{8,10},{9,11},{10,... | collective-permute-start | bytes 1966088 | tf_op jit(solution)/shard_map/ppermute | solution.py:64
  73.0 30.5 %collective-permute-start.17 = (bf16[640,512]{1,0:T(8,128)(2,1)S(1)}, bf16[640,512]{1,0:T(8,128)(2,1)S(1)}, u32[]{:S(2)}, u32[]{:S(2)}) collective-permute-start(bf16[640,512]{1,0:T(8,128)(2,1)S(1)} %pad_maximum_fusion.7.refs_0_), channel_id=1, source_target_pairs={{0,3},{1,0},{2,1},{3,2},{4,7},{5,4},{6,5},{7,6},{8,11},{9,8},{10,9... | collective-permute-start | bytes 1966088 | tf_op jit(solution)/shard_map/ppermute | solution.py:64
  74.3 16.3 %collective-permute-start.15 = (bf16[256,1024]{1,0:T(8,128)(2,1)S(1)}, bf16[256,1024]{1,0:T(8,128)(2,1)S(1)}, u32[]{:S(2)}, u32[]{:S(2)}) collective-permute-start(bf16[256,1024]{1,0:T(8,128)(2,1)S(1)} %pad_maximum_fusion.8), channel_id=1, source_target_pairs={{0,64},{4,20},{8,72},{12,28},{16,80},{20,4},{24,88},{28,12},{32,96... | collective-permute-start | bytes 1572872 | tf_op jit(solution)/shard_map/ppermute | solution.py:64
  75.4 26.2 %collective-permute-start.14 = (bf16[256,1024]{1,0:T(8,128)(2,1)S(1)}, bf16[256,1024]{1,0:T(8,128)(2,1)S(1)}, u32[]{:S(2)}, u32[]{:S(2)}) collective-permute-start(bf16[256,1024]{1,0:T(8,128)(2,1)S(1)} %pad_maximum_fusion.8), channel_id=1, source_target_pairs={{0,96},{4,28},{8,104},{12,4},{16,112},{20,12},{24,120},{28,20},{32... | collective-permute-start | bytes 1572872 | tf_op jit(solution)/shard_map/ppermute | solution.py:64
  108.8 145.8 %reduce-scatter.5.cloned.1.call-start = ((), (), s32[]{:S(2)}) async-start(), calls=%async_computation.5 | async-start | bytes 5242880 | tf_op jit(solution)/shard_map/reduce_scatter | solution.py:460
  109.1 18.9 %collective-permute-start.13 = (bf16[640,1024]{1,0:T(8,128)(2,1)S(1)}, bf16[640,1024]{1,0:T(8,128)(2,1)S(1)}, u32[]{:S(2)}, u32[]{:S(2)}) collective-permute-start(bf16[640,1024]{1,0:T(8,128)(2,1)S(1)} %pad_maximum_fusion.1.refs_0_), channel_id=1, source_target_pairs={{0,1},{1,2},{2,3},{3,0},{4,7},{5,4},{6,5},{7,6},{8,9},{9,10},{10,1... | collective-permute-start | bytes 3932168 | tf_op jit(solution)/shard_map/ppermute | solution.py:75
  113.5 14.5 %collective-permute-start.20 = (bf16[320,2048]{1,0:T(8,128)(2,1)S(1)}, bf16[320,2048]{1,0:T(8,128)(2,1)S(1)}, u32[]{:S(2)}, u32[]{:S(2)}) collective-permute-start(bf16[320,2048]{1,0:T(8,128)(2,1)S(1)} %get-tuple-element.109), channel_id=1, source_target_pairs={{0,4},{4,0},{8,12},{12,8},{16,20},{20,16},{24,28},{28,24},{32,36},... | collective-permute-start | bytes 3932168 | tf_op jit(solution)/shard_map/ppermute | solution.py:92
  128.0 18.8 %collective-permute-start.21 = (bf16[640,1024]{1,0:T(8,128)(2,1)S(1)}, bf16[640,1024]{1,0:T(8,128)(2,1)S(1)}, u32[]{:S(2)}, u32[]{:S(2)}) collective-permute-start(bf16[640,1024]{1,0:T(8,128)(2,1)S(1)} %collective-permute-done.13.refs_1_), channel_id=1, source_target_pairs={{0,1},{1,2},{2,3},{3,0},{4,7},{5,4},{6,5},{7,6},{8,9},{9,10},{10,1... | collective-permute-start | bytes 3932168 | tf_op jit(solution)/shard_map/ppermute | solution.py:75
  146.8 19.9 %collective-permute-start.23 = (bf16[320,4096]{1,0:T(8,128)(2,1)S(1)}, bf16[320,4096]{1,0:T(8,128)(2,1)S(1)}, u32[]{:S(2)}, u32[]{:S(2)}) collective-permute-start(bf16[320,4096]{1,0:T(8,128)(2,1)S(1)} %get-tuple-element.123), channel_id=1, source_target_pairs={{0,4},{4,0},{8,12},{12,8},{16,20},{20,16},{24,28},{28,24},{32,36},... | collective-permute-start | bytes 7864328 | tf_op jit(solution)/shard_map/ppermute | solution.py:92
  146.8 18.8 %collective-permute-start.22 = (bf16[640,1024]{1,0:T(8,128)(2,1)S(1)}, bf16[640,1024]{1,0:T(8,128)(2,1)S(1)}, u32[]{:S(2)}, u32[]{:S(2)}) collective-permute-start(bf16[640,1024]{1,0:T(8,128)(2,1)S(1)} %collective-permute-done.21.refs_2_), channel_id=1, source_target_pairs={{0,1},{1,2},{2,3},{3,0},{4,7},{5,4},{6,5},{7,6},{8,9},{9,10},{10,1... | collective-permute-start | bytes 3932168 | tf_op jit(solution)/shard_map/ppermute | solution.py:75
  218.5 78.3 %reduce-scatter.3.cloned.1.call-start = ((), (), s32[]{:S(2)}) async-start(), calls=%async_computation.4 | async-start | bytes 10485760 | tf_op jit(solution)/shard_map/reduce_scatter | solution.py:460
  219.6 32.3 %collective-permute-start.25 = (bf16[640,512]{1,0:T(8,128)(2,1)S(1)}, bf16[640,512]{1,0:T(8,128)(2,1)S(1)}, u32[]{:S(2)}, u32[]{:S(2)}) collective-permute-start(bf16[640,512]{1,0:T(8,128)(2,1)S(1)} %copy-done.27), channel_id=1, source_target_pairs={{0,1},{1,2},{2,3},{3,0},{4,5},{5,6},{6,7},{7,4},{8,9},{9,10},{10,1... | collective-permute-start | bytes 1966088 | tf_op jit(solution)/shard_map/ppermute | solution.py:81
  219.8 32.1 %collective-permute-start.26 = (bf16[640,512]{1,0:T(8,128)(2,1)S(1)}, bf16[640,512]{1,0:T(8,128)(2,1)S(1)}, u32[]{:S(2)}, u32[]{:S(2)}) collective-permute-start(bf16[640,512]{1,0:T(8,128)(2,1)S(1)} %copy-done.25), channel_id=1, source_target_pairs={{0,2},{1,3},{2,0},{3,1},{4,6},{5,7},{6,4},{7,5},{8,10},{9,11},{10,... | collective-permute-start | bytes 1966088 | tf_op jit(solution)/shard_map/ppermute | solution.py:81
  221.6 30.9 %collective-permute-start.27 = (bf16[640,512]{1,0:T(8,128)(2,1)S(1)}, bf16[640,512]{1,0:T(8,128)(2,1)S(1)}, u32[]{:S(2)}, u32[]{:S(2)}) collective-permute-start(bf16[640,512]{1,0:T(8,128)(2,1)S(1)} %copy-done.23), channel_id=1, source_target_pairs={{0,3},{1,0},{2,1},{3,2},{4,7},{5,4},{6,5},{7,6},{8,11},{9,8},{10,9... | collective-permute-start | bytes 1966088 | tf_op jit(solution)/shard_map/ppermute | solution.py:81
  299.0 22.6 %collective-permute-start.33 = (bf16[256,1536]{1,0:T(8,128)(2,1)S(1)}, bf16[256,1536]{1,0:T(8,128)(2,1)S(1)}, u32[]{:S(2)}, u32[]{:S(2)}) collective-permute-start(bf16[256,1536]{1,0:T(8,128)(2,1)S(1)} %pad_maximum_fusion.4), channel_id=1, source_target_pairs={{0,32},{4,12},{8,40},{12,20},{16,48},{20,28},{24,56},{28,4},{32,64... | collective-permute-start | bytes 2359304 | tf_op jit(solution)/shard_map/ppermute | solution.py:81
  300.3 24.8 %collective-permute-start.34 = (bf16[256,1536]{1,0:T(8,128)(2,1)S(1)}, bf16[256,1536]{1,0:T(8,128)(2,1)S(1)}, u32[]{:S(2)}, u32[]{:S(2)}) collective-permute-start(bf16[256,1536]{1,0:T(8,128)(2,1)S(1)} %pad_maximum_fusion.5), channel_id=1, source_target_pairs={{0,64},{4,20},{8,72},{12,28},{16,80},{20,4},{24,88},{28,12},{32,96... | collective-permute-start | bytes 2359304 | tf_op jit(solution)/shard_map/ppermute | solution.py:81
  301.2 26.1 %collective-permute-start.35 = (bf16[256,1536]{1,0:T(8,128)(2,1)S(1)}, bf16[256,1536]{1,0:T(8,128)(2,1)S(1)}, u32[]{:S(2)}, u32[]{:S(2)}) collective-permute-start(bf16[256,1536]{1,0:T(8,128)(2,1)S(1)} %pad_maximum_fusion.6), channel_id=1, source_target_pairs={{0,96},{4,28},{8,104},{12,4},{16,112},{20,12},{24,120},{28,20},{32... | collective-permute-start | bytes 2359304 | tf_op jit(solution)/shard_map/ppermute | solution.py:81
  303.2 15.3 %collective-permute-start.31 = (bf16[256,512]{1,0:T(8,128)(2,1)S(1)}, bf16[256,512]{1,0:T(8,128)(2,1)S(1)}, u32[]{:S(2)}, u32[]{:S(2)}) collective-permute-start(bf16[256,512]{1,0:T(8,128)(2,1)S(1)} %get-tuple-element.154), channel_id=1, source_target_pairs={{0,16},{4,68},{8,24},{12,76},{16,0},{20,84},{24,8},{28,92},{32,48}... | collective-permute-start | bytes 786440 | tf_op jit(solution)/shard_map/ppermute | solution.py:81
  327.8 13.4 %collective-permute-start.41 = (bf16[64,1536]{1,0:T(8,128)(2,1)S(1)}, bf16[64,1536]{1,0:T(8,128)(2,1)S(1)}, u32[]{:S(2)}, u32[]{:S(2)}) collective-permute-start(bf16[64,1536]{1,0:T(8,128)(2,1)S(1)} %get-tuple-element.182), channel_id=1, source_target_pairs={{0,3},{1,0},{2,1},{3,2},{4,7},{5,4},{6,5},{7,6},{8,11},{9,8},{10,9... | collective-permute-start | bytes 589832 | tf_op jit(solution)/shard_map/ppermute | solution.py:81
  330.8 10.4 %collective-permute-start.40 = (bf16[64,1536]{1,0:T(8,128)(2,1)S(1)}, bf16[64,1536]{1,0:T(8,128)(2,1)S(1)}, u32[]{:S(2)}, u32[]{:S(2)}) collective-permute-start(bf16[64,1536]{1,0:T(8,128)(2,1)S(1)} %get-tuple-element.183), channel_id=1, source_target_pairs={{0,2},{1,3},{2,0},{3,1},{4,6},{5,7},{6,4},{7,5},{8,10},{9,11},{10,... | collective-permute-start | bytes 589832 | tf_op jit(solution)/shard_map/ppermute | solution.py:81
  (59 other events, 418.8 us)
Sparse Core Ops, SparseCore 0:
  60.2 45.4 all-gather.2
  108.9 50.2 all-gather.4
  218.6 28.7 reduce-scatter.4
  249.8 46.9 reduce-scatter.2
